TPU v7x, 32 devices: a whole 2x2x4 slice. The times are simulated.
32 devices in a mesh: dap: 16 (over z, y, x), rep: 2 (over core).
Axes of the slice: x: 2, y: 2, z: 4, core: 2. Of those that a mesh axis runs over, the one named last changes fastest.
Arguments:
- pair: bfloat16 [256, 128, 128], P(('rep', 'dap')), parts along dimension 0, may hold values from -6 to 6
- w_proj: bfloat16 [128, 512], replicated, may hold values from -0.5 to 0.5
- w_gate_out: bfloat16 [128, 128], replicated, may hold values from -0.5 to 0.5
- w_out: bfloat16 [128, 128], replicated, may hold values from -0.5 to 0.5
- w_qkvg: bfloat16 [128, 512], replicated, may hold values from -0.5 to 0.5
- w_bias: bfloat16 [128, 4], replicated
- w_att_out: bfloat16 [128, 128], replicated, may hold values from -0.5 to 0.5
- length: int32 [2], P('rep'), parts along dimension 0, may hold values from 64 to 128
Outputs:
- pair_out: bfloat16 [256, 128, 128], P('rep', 'dap'), parts along dimension 0
There are 2 independent parts, one for each index of `rep`. A program takes and returns all parts, laid end to end along the dimension named above; an argument that names none is the same for every part. Nothing has to cross between parts.
All inputs are finite; a program needn't handle non-finite values.
Results may differ from a plain program's by a relative error of at most 0.017.
The roundings to bfloat16 on the way count: a program that leaves them out, or rounds other values in their place, can miss the bound.
Values may be sent and summed in bfloat16 or wider, within the bound.
No kernel may reach another device: no remote copies, remote signals or barrier semaphores. Data moves between devices by JAX's collectives and lax.ppermute only.
A program may use at most 192 MiB of HBM per device.

v0:
```python
import jax
import jax.numpy as jnp
from jax import lax
from jax.sharding import PartitionSpec as P


def layer_norm(x, axis):
    mean = jnp.mean(x, axis=axis, keepdims=True)
    centered = x - mean
    spread = jnp.mean(centered * centered, axis=axis, keepdims=True)
    return centered * lax.rsqrt(spread + 1e-05)


def body(pair, w_proj, w_gate_out, w_out, w_qkvg, w_bias, w_att_out, length):
    row_count, full_count, channels = pair.shape
    hidden = w_out.shape[0]
    my_index = lax.axis_index("dap")
    positions = jnp.arange(full_count, dtype=jnp.int32)
    valid_keys = (positions < length[0]).astype(jnp.float32)
    row_valid = lax.dynamic_slice_in_dim(valid_keys, my_index * row_count, row_count)
    normed = layer_norm(pair.astype(jnp.float32), 2).astype(jnp.bfloat16)
    projected = jnp.einsum("rnc,ce->ern", normed, w_proj, preferred_element_type=jnp.float32)
    pair_mask = row_valid[:, None] * valid_keys[None, :]
    left_terms = (
        jax.nn.sigmoid(projected[hidden : 2 * hidden]) * projected[:hidden] * pair_mask[None]
    ).astype(jnp.bfloat16)
    right_terms = (
        jax.nn.sigmoid(projected[3 * hidden :])
        * projected[2 * hidden : 3 * hidden]
        * pair_mask[None]
    ).astype(jnp.bfloat16)
    product = jnp.einsum(
        "cik,cjk->cij",
        left_terms,
        lax.all_gather(right_terms, "dap", axis=1, tiled=True),
        preferred_element_type=jnp.float32,
    )
    product_norm = layer_norm(product, 0).astype(jnp.bfloat16)
    update = jnp.einsum("cij,cd->ijd", product_norm, w_out, preferred_element_type=jnp.float32)
    gate_out = jax.nn.sigmoid(
        jnp.einsum("ijc,cd->ijd", normed, w_gate_out, preferred_element_type=jnp.float32)
    )
    pair_rows = (pair.astype(jnp.float32) + gate_out * update).astype(jnp.bfloat16)
    columns = lax.all_to_all(pair_rows, "dap", split_axis=1, concat_axis=0, tiled=True)
    normed_mid = layer_norm(columns.astype(jnp.float32), 2).astype(jnp.bfloat16)
    bias_local = jnp.einsum(
        "kic,ch->hki", normed_mid, w_bias, preferred_element_type=jnp.float32
    ).astype(jnp.bfloat16)
    bias_whole = lax.all_gather(bias_local, "dap", axis=2, tiled=True)
    bias_turned = jnp.transpose(bias_whole, (0, 2, 1)).astype(jnp.float32)
    heads = w_bias.shape[1]
    width = w_att_out.shape[0]
    head_size = width // heads
    mixed = jnp.einsum("ijc,ce->ije", normed_mid, w_qkvg, preferred_element_type=jnp.float32)
    queries = (
        mixed[..., :width].astype(jnp.bfloat16).reshape(full_count, row_count, heads, head_size)
    )
    keys_local = (
        mixed[..., width : 2 * width]
        .astype(jnp.bfloat16)
        .reshape(full_count, row_count, heads, head_size)
    )
    values_local = (
        mixed[..., 2 * width : 3 * width]
        .astype(jnp.bfloat16)
        .reshape(full_count, row_count, heads, head_size)
    )
    gate = jax.nn.sigmoid(mixed[..., 3 * width :])
    score = jnp.einsum(
        "ijhd,kjhd->jhik", queries, keys_local, preferred_element_type=jnp.float32
    ) * head_size ** (-0.5)
    score = score + bias_turned[None]
    score = jnp.where(valid_keys[None, None, None, :] > 0, score, -1000000000.0)
    top = jnp.max(score, axis=3, keepdims=True)
    expo = jnp.exp(score - top)
    weights = (expo / jnp.sum(expo, axis=3, keepdims=True)).astype(jnp.bfloat16)
    output = jnp.einsum(
        "jhik,kjhd->ijhd", weights, values_local, preferred_element_type=jnp.float32
    )
    attended = (gate * output.reshape(full_count, row_count, width)).astype(jnp.bfloat16)
    result = columns.astype(jnp.float32) + jnp.einsum(
        "ije,ec->ijc", attended, w_att_out, preferred_element_type=jnp.float32
    )
    return result.astype(jnp.bfloat16)


def solution(mesh):
    placed = (P(("rep", "dap"), None, None), P(), P(), P(), P(), P(), P(), P("rep"))
    return jax.shard_map(
        body, mesh=mesh, in_specs=placed, out_specs=P("rep", "dap", None), check_vma=False
    )
```

profile of v0, /device:TPU:0, one launch (start us, length us, event | category | flops | bytes accessed | tf_op | source)
XLA Modules:
  0.0 170.9 jit_solution(5762942910309972968)
XLA Ops:
  7.2 0.1 dynamic_slice.3
  7.3 0.1 broadcast_multiply_fusion.1
  7.4 1.1 convert_reduce_fusion
  8.5 1.3 fusion.18
  9.8 1.5 convolution_bitcast_fusion
  11.3 0.0 copy-start.1
  11.3 0.0 copy-start.7
  11.3 0.3 fusion.21
  11.7 0.9 copy.53
  12.5 0.0 all-gather.2.cloned.1.call-update
  12.5 0.2 copy.54
  12.8 0.7 fusion.6
  13.5 0.0 copy-start.5
  13.5 78.0 %all-gather.2.cloned.1.call-done = bf16[128,128,128]{2,0,1:T(8,128)(2,1)} async-done(((bf16[128,8,128]{2,0,1:T(8,128)(2,1)}), bf16[128,128,128]{2,0,1:T(8,128)(2,1)}) %all-gather.2.cloned.1.call-update) | async-done | bytes 4194320 | tf_op jit(solution)/shard_map/all_gather | solution.py:35
  91.5 5.7 %fusion.52 = (f32[8,128]{1,0:T(8,128)S(1)}, f32[128,8,128]{2,1,0:T(8,128)S(1)}) fusion(bf16[128,8,128]{2,1,0:T(8,128)(2,1)S(1)} %copy.54, bf16[128,128,128]{2,0,1:T(8,128)(2,1)} %all-gather.2.cloned.1.call-done), kind=kOutput, calls=%fused_computation.79 | convolution fusion | flops 33684480 | bytes 4984832 | tf_op jit(solution)/shard_map/cik,cjk->cij/dot_general | solution.py:32
  97.2 0.1 multiply_reduce_fusion
  97.3 0.1 multiply_convert_fusion
  97.4 0.3 fusion.8
  97.7 0.0 copy-start.6
  97.7 0.9 copy.57
  98.6 4.2 %all-to-all-start = ((bf16[8,128,128]{2,0,1:T(8,128)(2,1)}), bf16[8,128,128]{2,0,1:T(8,128)(2,1)S(1)}, u32[]{:S(2)}, u32[]{:S(2)}) async-start(bf16[8,128,128]{2,0,1:T(8,128)(2,1)} %copy.57), calls=%async_computation | async-start | bytes 524288 | tf_op jit(solution)/shard_map/all_to_all | solution.py:44
  102.8 9.9 %all-to-all-done = bf16[8,128,128]{2,0,1:T(8,128)(2,1)S(1)} async-done(((bf16[8,128,128]{2,0,1:T(8,128)(2,1)}), bf16[8,128,128]{2,0,1:T(8,128)(2,1)S(1)}, u32[]{:S(2)}, u32[]{:S(2)}) %all-to-all-start) | async-done | bytes 262176 | tf_op jit(solution)/shard_map/all_to_all | solution.py:44
  112.7 0.1 bitcast_convert_fusion
  112.7 0.2 bitcast_reduce_fusion
  113.0 0.1 copy.60
  113.0 0.1 copy.62
  113.1 0.1 copy.61
  113.2 0.4 fusion.34
  113.6 0.1 copy.63
  113.7 0.1 copy.64
  113.8 0.1 rsqrt.30
  113.9 0.1 div.48
  114.0 0.5 fusion.10
  114.5 38.4 %all_gather.7 = bf16[4,128,128]{1,0,2:T(4,128)(2,1)S(1)} all-gather(bf16[4,128,8]{1,0,2:T(4,128)(2,1)S(1)} %fusion.10), channel_id=1, replica_groups=mesh['dap'=16,'rep'=2] {'dap'}, dimensions={2}, use_global_device_ids=true | all-gather | bytes 139264 | tf_op jit(solution)/shard_map/all_gather | solution.py:49
  152.9 0.8 copy.69
  153.8 0.5 fusion.53
  154.3 0.2 fusion.51
  154.5 0.9 copy.68
  155.3 0.9 copy.67
  156.2 0.8 copy.66
  157.1 0.1 slice.39
  157.1 0.2 copy.76
  157.3 0.0 copy-start.3
  157.3 3.4 %fusion.54 = (f32[8,4,128]{2,1,0:T(4,128)S(1)}, f32[8,4,128,128]{2,3,1,0:T(8,128)}) fusion(f32[4,128,128]{1,2,0:T(8,128)S(1)} %copy-done.2, pred[128]{0:T(512)(128)(4,1)S(1)} %broadcast_compare_fusion, bf16[128,8,4,32]{0,3,2,1:T(8,128)(2,1)} %bitcast.72, bf16[128,8,4,32]{0,3,2,1:T(8,128)(2,1)} %bitcast.71), kind=kOutput, calls=%fused_computation.81 | convolution fusion | flops 36176000 | bytes 2900096 | tf_op jit(solution)/shard_map/sub | solution.py:75
  160.7 2.0 %fusion.15 = f32[8,4,32,128]{3,2,1,0:T(8,128)S(1)} fusion(bf16[128,8,4,32]{0,3,2,1:T(8,128)(2,1)S(1)} %bitcast.73, f32[8,4,128,128]{2,3,1,0:T(8,128)} %get-tuple-element.17, f32[8,4,128]{2,1,0:T(4,128)S(1)} %get-tuple-element.16), kind=kOutput, calls=%fused_computation.23 | convolution fusion | flops 34603008 | bytes 2899968 | tf_op jit(solution)/shard_map/jhik,kjhd->ijhd/dot_general | solution.py:77
  162.7 0.1 fusion.30
  162.9 0.3 fusion.9
  163.2 0.9 copy.72
  (21 shorter events, 0.1 us)
Async XLA Ops:
  6.5 147.2 %copy-start = (bf16[128,512]{1,0:T(8,128)(2,1)S(1)}, bf16[128,512]{1,0:T(8,128)(2,1)}, u32[]{:S(2)}) copy-start(bf16[128,512]{1,0:T(8,128)(2,1)} %param.12) | copy-start | bytes 393220
  6.5 84.9 %all-gather.2.cloned.1.call-start = ((), (), s32[]{:S(2)}) async-start(), calls=%async_computation.1 | async-start | bytes 4456448 | tf_op jit(solution)/shard_map/all_gather | solution.py:35
  11.3 1.4 copy-start.1
  11.3 1.4 copy-start.7
  13.5 83.9 %copy-start.5 = (bf16[128,128]{1,0:T(8,128)(2,1)S(1)}, bf16[128,128]{1,0:T(8,128)(2,1)}, u32[]{:S(2)}) copy-start(bf16[128,128]{1,0:T(8,128)(2,1)} %param.11) | copy-start | bytes 98308
  97.7 16.3 %copy-start.6 = (bf16[128,4]{0,1:T(4,128)(2,1)S(1)}, bf16[128,4]{0,1:T(4,128)(2,1)}, u32[]{:S(2)}) copy-start(bf16[128,4]{0,1:T(4,128)(2,1)} %param.13) | copy-start | bytes 3076
  98.6 14.1 %all-to-all-start = ((bf16[8,128,128]{2,0,1:T(8,128)(2,1)}), bf16[8,128,128]{2,0,1:T(8,128)(2,1)S(1)}, u32[]{:S(2)}, u32[]{:S(2)}) async-start(bf16[8,128,128]{2,0,1:T(8,128)(2,1)} %copy.57), calls=%async_computation | async-start | bytes 524288 | tf_op jit(solution)/shard_map/all_to_all | solution.py:44
  155.3 2.0 %copy-start.2 = (f32[4,128,128]{1,2,0:T(8,128)S(1)}, f32[4,128,128]{1,2,0:T(8,128)}, u32[]{:S(2)}) copy-start(f32[4,128,128]{1,2,0:T(8,128)} %copy.69) | copy-start | bytes 786436
  157.3 3.4 %copy-start.3 = (bf16[128,8,128]{0,2,1:T(8,128)(2,1)S(1)}, bf16[128,8,128]{0,2,1:T(8,128)(2,1)}, u32[]{:S(2)}) copy-start(bf16[128,8,128]{0,2,1:T(8,128)(2,1)} %copy.66) | copy-start | bytes 786436
  160.7 2.2 %copy-start.4 = (bf16[128,128]{1,0:T(8,128)(2,1)S(1)}, bf16[128,128]{1,0:T(8,128)(2,1)}, u32[]{:S(2)}) copy-start(bf16[128,128]{1,0:T(8,128)(2,1)} %param.14) | copy-start | bytes 98308
Sparse Core Ops, SparseCore 0:
  12.7 78.7 all-gather.1
where the time goes:
time: 171 us
  waiting for transfers between devices  87.8 us (51%)
  blocking collectives  38.4 us (22%)
  matrix products  14.7 us (9%)
  between operations  14.3 us (8%)
  local copies, waits for them, and re-layouts  7.39 us (4%)
  starting transfers between devices  4.22 us (2%)
  other arithmetic  3.93 us (2%)
    all_gather x1, waiting for transfers between devices, body(): lax.all_gather(right_terms, 'dap', axis=1, tiled=True)  78 us
    all_gather x1, blocking collectives, body(): bias_whole = lax.all_gather(bias_local, 'dap', axis=2, tiled=True)  38.4 us
    all_to_all x1, waiting for transfers between devices, body(): lax.all_to_all(pair_rows, 'dap', split_axis=1, concat_axis=0, tiled=True)  9.86 us
    dot_general x1, matrix products, body(): jnp.einsum('cik,cjk->cij', left_terms, lax.all_gather(right_terms, 'dap',...  5.71 us
    all_to_all x1, starting transfers between devices, body(): lax.all_to_all(pair_rows, 'dap', split_axis=1, concat_axis=0, tiled=True)  4.22 us
  transfers between devices with their start and end apart: 2, of which 2 were waited for; matrix products, arithmetic and copies ran while one was open for 1% of the time, Pallas kernels for 0%

commit v1 on v0

v1 whole, which is shorter than its diff:
```python
import jax
import jax.numpy as jnp
from jax import lax
from jax.sharding import PartitionSpec as P


def layer_norm(x, axis):
    mean = jnp.mean(x, axis=axis, keepdims=True)
    centered = x - mean
    spread = jnp.mean(centered * centered, axis=axis, keepdims=True)
    return centered * lax.rsqrt(spread + 1e-05)


def exchange(x):
    return lax.all_to_all(x, "dap", split_axis=0, concat_axis=0, tiled=True)


def matmul(spec, a, b):
    return jnp.einsum(spec, a, b, preferred_element_type=jnp.float32)


def body(pair, w_proj, w_gate_out, w_out, w_qkvg, w_bias, w_att_out, length):
    row_count, full_count, channels = pair.shape
    hidden = w_out.shape[0]
    device_count = full_count // row_count
    share = hidden // device_count
    my_index = lax.axis_index("dap")
    positions = jnp.arange(full_count, dtype=jnp.int32)
    valid_keys = (positions < length[0]).astype(jnp.float32)
    row_valid = lax.dynamic_slice_in_dim(valid_keys, my_index * row_count, row_count)

    normed = layer_norm(pair.astype(jnp.float32), 2).astype(jnp.bfloat16)
    projected = matmul("rnc,ce->ern", normed, w_proj)
    pair_mask = row_valid[:, None] * valid_keys[None, :]
    left = jax.nn.sigmoid(projected[hidden : 2 * hidden]) * projected[:hidden] * pair_mask
    right = jax.nn.sigmoid(projected[3 * hidden :]) * projected[2 * hidden : 3 * hidden] * pair_mask
    blocks = (device_count, share * row_count, full_count)
    left = left.astype(jnp.bfloat16).reshape(blocks)
    right = right.astype(jnp.bfloat16).reshape(blocks)
    columns = jnp.transpose(
        pair.reshape(row_count, device_count, row_count, channels), (1, 0, 2, 3)
    )
    cut = share * row_count * full_count
    sent = jnp.concatenate(
        [
            left.reshape(device_count, cut),
            right.reshape(device_count, cut),
            columns.reshape(device_count, row_count * row_count * channels),
        ],
        axis=1,
    )
    came = exchange(sent.reshape(device_count, -1, channels)).reshape(device_count, -1)
    rows = (device_count, share, row_count, full_count)
    left = jnp.transpose(came[:, :cut].reshape(rows), (1, 0, 2, 3))
    right = jnp.transpose(came[:, cut : 2 * cut].reshape(rows), (1, 0, 2, 3))
    columns = came[:, 2 * cut :].reshape(full_count, row_count, channels)

    square = (share, full_count, full_count)
    product = matmul("cjk,cik->cji", right.reshape(square), left.reshape(square))
    product = product.astype(jnp.bfloat16).reshape(share, device_count, row_count, full_count)
    product = exchange(jnp.transpose(product, (1, 0, 2, 3)))
    product = product.reshape(hidden, row_count, full_count)
    product_norm = layer_norm(product.astype(jnp.float32), 0).astype(jnp.bfloat16)
    update = matmul("cji,cd->ijd", product_norm, w_out)
    normed = layer_norm(columns.astype(jnp.float32), 2).astype(jnp.bfloat16)
    gate_out = jax.nn.sigmoid(matmul("ijc,cd->ijd", normed, w_gate_out))
    columns = (columns.astype(jnp.float32) + gate_out * update).astype(jnp.bfloat16)

    normed_mid = layer_norm(columns.astype(jnp.float32), 2).astype(jnp.bfloat16)
    heads = w_bias.shape[1]
    width = w_att_out.shape[0]
    head_size = width // heads
    bias = matmul("kic,ch->hik", normed_mid, w_bias).astype(jnp.bfloat16)
    bias = exchange(jnp.broadcast_to(bias[None], (device_count,) + bias.shape))
    bias = jnp.transpose(bias, (1, 0, 2, 3)).reshape(heads, full_count, full_count)

    mixed = matmul("ijc,ce->ije", normed_mid, w_qkvg)
    per_head = (full_count, row_count, heads, head_size)
    queries = mixed[..., :width].astype(jnp.bfloat16).reshape(per_head)
    keys = mixed[..., width : 2 * width].astype(jnp.bfloat16).reshape(per_head)
    values = mixed[..., 2 * width : 3 * width].astype(jnp.bfloat16).reshape(per_head)
    gate = jax.nn.sigmoid(mixed[..., 3 * width :])
    score = matmul("ijhd,kjhd->jhik", queries, keys) * head_size ** (-0.5)
    score = score + bias.astype(jnp.float32)[None]
    score = jnp.where(valid_keys > 0, score, -1000000000.0)
    top = jnp.max(score, axis=3, keepdims=True)
    expo = jnp.exp(score - top)
    weights = (expo / jnp.sum(expo, axis=3, keepdims=True)).astype(jnp.bfloat16)
    output = matmul("jhik,kjhd->ijhd", weights, values)
    attended = (gate * output.reshape(full_count, row_count, width)).astype(jnp.bfloat16)
    result = columns.astype(jnp.float32) + matmul("ije,ec->ijc", attended, w_att_out)
    return result.astype(jnp.bfloat16)


def solution(mesh):
    placed = (P(("rep", "dap"), None, None), P(), P(), P(), P(), P(), P(), P("rep"))
    return jax.shard_map(
        body, mesh=mesh, in_specs=placed, out_specs=P("rep", "dap", None), check_vma=False
    )
```

time: 171 us -> 72.5 us (0.42)
  waiting for transfers between devices: 87.8 us -> 30.5 us
  blocking collectives: 38.4 us -> 0 us
  between operations: 14.3 us -> 1.01 us
  starting transfers between devices: 4.22 us -> 17.4 us
  matrix products: 14.7 us -> 8.58 us
  other arithmetic: 3.93 us -> 6.27 us
    all_gather x1 -> x0, waiting for transfers between devices: 78 us -> none  [body(): lax.all_gather(right_terms, 'dap', axis=1, tiled=True)]
    all_gather x1 -> x0, blocking collectives: 38.4 us -> none  [body(): bias_whole = lax.all_gather(bias_local, 'dap', axis=2, tiled=True)]
    all_to_all x1 -> x3, waiting for transfers between devices: 9.86 us -> 30.5 us  [exchange(): return lax.all_to_all(x, 'dap', split_axis=0, concat_axis=0, tiled=True)]
    all_to_all x1 -> x3, starting transfers between devices: 4.22 us -> 17.4 us  [exchange(): return lax.all_to_all(x, 'dap', split_axis=0, concat_axis=0, tiled=True)]
    dot_general x8, matrix products: 11.4 us -> 5.28 us  [matmul(): return jnp.einsum(spec, a, b, preferred_element_type=jnp.float32)]
    convert_element_type x4 -> x6, local copies, waits for them, and re-layouts: 2.75 us -> 0.82 us  [the longest x2 0.31 us: body(): columns.astype(jnp.float32) + gate_out * update]
  transfers between devices with their start and end apart: 2 -> 3, of which waited for: 2 -> 3; matrix products, arithmetic and copies ran while one was open for 1% -> 8% of each run, Pallas kernels for 0% -> 0%
where the time goes in v1:
time: 72.5 us; the launch traced here: 72 us
  waiting for transfers between devices  30.5 us (42%)
  starting transfers between devices  17.4 us (24%)
  matrix products  8.58 us (12%)
  local copies, waits for them, and re-layouts  8.24 us (11%)
  other arithmetic  6.27 us (9%)
  between operations  1.01 us (1%)
    all_to_all x3, waiting for transfers between devices, exchange(): return lax.all_to_all(x, 'dap', split_axis=0, concat_axis=0, tiled=True)  30.5 us
    all_to_all x3, starting transfers between devices, exchange(): return lax.all_to_all(x, 'dap', split_axis=0, concat_axis=0, tiled=True)  17.4 us
    dot_general x8, matrix products, matmul(): return jnp.einsum(spec, a, b, preferred_element_type=jnp.float32)  5.28 us
    sub x1, matrix products, body(): expo = jnp.exp(score - top)  3.3 us
    reduce_sum x4, other arithmetic, layer_norm(): spread = jnp.mean(centered * centered, axis=axis, keepdims=True)  1.89 us
    reduce_sum x3, other arithmetic, layer_norm(): mean = jnp.mean(x, axis=axis, keepdims=True)  1.47 us
  transfers between devices with their start and end apart: 3, of which 3 were waited for; matrix products, arithmetic and copies ran while one was open for 8% of the time, Pallas kernels for 0%

profile of v1, /device:TPU:0, one launch (start us, length us, event | category | flops | bytes accessed | tf_op | source)
XLA Modules:
  0.0 72.0 jit_solution(14416763590860997546)
XLA Ops:
  0.0 1.1 %convert_reduce_fusion = f32[8,128]{1,0:T(8,128)S(1)} fusion(bf16[8,128,128]{2,1,0:T(8,128)(2,1)} %param.8), kind=kLoop, calls=%fused_computation.29 | loop fusion | flops 261120 | bytes 266240 | tf_op jit(solution)/shard_map/reduce_sum | solution.py:8
  1.1 1.0 %copy_bitcast_fusion.2 = bf16[16,64,128]{2,1,0:T(8,128)(2,1)S(1)} fusion(bf16[8,128,128]{2,1,0:T(8,128)(2,1)} %param.8), kind=kLoop, calls=%fused_computation.67 | loop fusion | bytes 524288 | tf_op jit(solution)/shard_map/concatenate | solution.py:44
  2.8 0.1 dynamic_slice.3
  2.9 0.1 broadcast_multiply_fusion.2
  3.0 1.3 %fusion.19 = f32[8,128]{1,0:T(8,128)S(1)} fusion(bf16[8,128,128]{2,1,0:T(8,128)(2,1)} %param.8, f32[8,128]{1,0:T(8,128)S(1)} %broadcast_multiply_fusion.4), kind=kLoop, calls=%fused_computation.32 | loop fusion | flops 523264 | bytes 270336 | tf_op jit(solution)/shard_map/reduce_sum | solution.py:10
  4.3 1.5 %convolution_bitcast_fusion = f32[512,8,128]{0,2,1:T(8,128)S(1)} fusion(bf16[8,128,128]{2,1,0:T(8,128)(2,1)} %param.8, f32[8,128]{1,0:T(8,128)S(1)} %add_rsqrt_fusion.3, f32[8,128]{1,0:T(8,128)S(1)} %broadcast_multiply_fusion.4, bf16[128,512]{1,0:T(8,128)(2,1)} %param.9), kind=kOutput, calls=%fused_computation.5 | convolution fusion | flops 134742016 | bytes 2498560 | tf_op jit(solution)/shard_map/rnc,ce->ern/dot_general | solution.py:19
  5.8 0.3 fusion.27
  6.1 0.2 copy.124
  6.3 0.2 copy.125
  6.5 0.9 %pad_maximum_fusion = bf16[16,192,128]{2,1,0:T(8,128)(2,1)} fusion(bf16[16,64,128]{2,1,0:T(8,128)(2,1)S(1)} %copy_bitcast_fusion.2, bf16[16,64,128]{2,1,0:T(8,128)(2,1)S(1)} %bitcast.100, bf16[16,64,128]{2,1,0:T(8,128)(2,1)S(1)} %bitcast.99), kind=kLoop, calls=%fused_computation.27 | loop fusion | flops 2359296 | bytes 1572864 | tf_op jit(solution)/shard_map/concatenate | solution.py:44
  7.4 8.3 %all-to-all-start = ((bf16[16,192,128]{2,1,0:T(8,128)(2,1)}), bf16[16,192,128]{2,1,0:T(8,128)(2,1)S(1)}, u32[]{:S(2)}, u32[]{:S(2)}) async-start(bf16[16,192,128]{2,1,0:T(8,128)(2,1)} %pad_maximum_fusion), calls=%async_computation | async-start | bytes 1572864 | tf_op jit(solution)/shard_map/all_to_all | solution.py:15
  15.8 19.7 %all-to-all-done = bf16[16,192,128]{2,1,0:T(8,128)(2,1)S(1)} async-done(((bf16[16,192,128]{2,1,0:T(8,128)(2,1)}), bf16[16,192,128]{2,1,0:T(8,128)(2,1)S(1)}, u32[]{:S(2)}, u32[]{:S(2)}) %all-to-all-start) | async-done | bytes 786464 | tf_op jit(solution)/shard_map/all_to_all | solution.py:15
  35.5 0.5 copy.187
  36.0 0.1 slice_bitcast_fusion.1
  36.2 0.3 fusion.10
  36.5 0.8 %copy.188 = bf16[8,16,8,128]{3,2,0,1:T(8,128)(2,1)} copy(bf16[8,16,8,128]{3,2,1,0:T(8,128)(2,1)S(1)} %fusion.10) | data formatting | bytes 524288 | tf_op jit(solution)/shard_map/reshape | solution.py:60
  37.3 4.9 %all-to-all-start.1 = ((bf16[16,8,8,128]{3,2,1,0:T(8,128)(2,1)}), bf16[16,8,8,128]{3,2,1,0:T(8,128)(2,1)S(1)}, u32[]{:S(2)}, u32[]{:S(2)}) async-start(bf16[16,8,8,128]{3,2,1,0:T(8,128)(2,1)} %bitcast.92), calls=%async_computation.1 | async-start | bytes 524288 | tf_op jit(solution)/shard_map/all_to_all | solution.py:15
  42.2 0.1 reshape.148
  42.3 0.2 copy.138
  42.5 0.2 reduce_sum.83
  42.8 0.1 copy.128
  42.9 0.4 multiply_reduce_fusion.2
  43.3 0.1 copy.130
  43.5 0.3 multiply_convert_fusion.1
  43.8 0.3 fusion.5
  44.2 6.5 %all-to-all-done.1 = bf16[16,8,8,128]{3,2,1,0:T(8,128)(2,1)S(1)} async-done(((bf16[16,8,8,128]{3,2,1,0:T(8,128)(2,1)}), bf16[16,8,8,128]{3,2,1,0:T(8,128)(2,1)S(1)}, u32[]{:S(2)}, u32[]{:S(2)}) %all-to-all-start.1) | async-done | bytes 262176 | tf_op jit(solution)/shard_map/all_to_all | solution.py:15
  50.7 0.1 convert_reduce_fusion.1
  50.8 0.1 multiply_reduce_fusion.1
  51.0 0.3 fusion.57
  51.3 0.1 multiply_reduce_fusion
  51.4 0.2 fusion.11
  51.6 0.7 broadcast_in_dim.9
  52.3 4.2 %all-to-all-start.2 = ((bf16[16,4,8,128]{3,2,1,0:T(8,128)(2,1)}), bf16[16,4,8,128]{3,2,1,0:T(8,128)(2,1)}, u32[]{:S(2)}, u32[]{:S(2)}) async-start(bf16[16,4,8,128]{3,2,1,0:T(8,128)(2,1)} %broadcast_in_dim.9), calls=%async_computation.2 | async-start | bytes 262144 | tf_op jit(solution)/shard_map/all_to_all | solution.py:15
  56.5 0.5 fusion.58
  56.9 0.2 fusion.56
  57.1 0.8 %copy.143 = bf16[128,8,128]{0,2,1:T(8,128)(2,1)} copy(bf16[128,8,128]{2,0,1:T(8,128)(2,1)S(1)} %get-tuple-element.7) | data formatting | bytes 524288 | tf_op jit(solution)/shard_map/slice | solution.py:80
  58.0 0.9 %copy.142 = bf16[128,8,128]{0,2,1:T(8,128)(2,1)} copy(bf16[128,8,128]{2,0,1:T(8,128)(2,1)S(1)} %get-tuple-element.8) | data formatting | bytes 524288 | tf_op jit(solution)/shard_map/slice | solution.py:79
  58.9 0.8 %copy.141 = bf16[128,8,128]{0,2,1:T(8,128)(2,1)} copy(bf16[128,8,128]{2,0,1:T(8,128)(2,1)S(1)} %get-tuple-element.9) | data formatting | bytes 524288 | tf_op jit(solution)/shard_map/slice | solution.py:81
  59.7 0.1 slice.54
  59.8 0.2 copy.161
  60.0 4.3 %all-to-all-done.2 = bf16[16,4,8,128]{3,2,1,0:T(8,128)(2,1)} async-done(((bf16[16,4,8,128]{3,2,1,0:T(8,128)(2,1)}), bf16[16,4,8,128]{3,2,1,0:T(8,128)(2,1)}, u32[]{:S(2)}, u32[]{:S(2)}) %all-to-all-start.2) | async-done | bytes 131104 | tf_op jit(solution)/shard_map/all_to_all | solution.py:15
  64.3 0.9 %convert_bitcast_fusion = f32[4,128,128]{2,1,0:T(8,128)S(1)} fusion(bf16[16,4,8,128]{3,2,1,0:T(8,128)(2,1)} %all-to-all-done.2), kind=kLoop, calls=%fused_computation.68 | loop fusion | flops 65536 | bytes 393216 | tf_op jit(solution)/shard_map/convert_element_type | solution.py:84
  65.2 0.1 copy.147
  65.3 3.3 %fusion.59 = (f32[8,4,128]{2,1,0:T(4,128)S(1)}, f32[8,4,128,128]{2,3,1,0:T(8,128)}) fusion(f32[4,128,128]{1,2,0:T(8,128)S(1)} %copy.147, pred[128]{0:T(512)(128)(4,1)S(1)} %broadcast_compare_fusion, bf16[128,8,4,32]{0,3,2,1:T(8,128)(2,1)} %bitcast.103, bf16[128,8,4,32]{0,3,2,1:T(8,128)(2,1)S(1)} %bitcast.101), kind=kOutput, calls=%fused_computation.98 | convolution fusion | flops 36176000 | bytes 2900096 | tf_op jit(solution)/shard_map/sub | solution.py:87
  68.6 2.0 %fusion.16 = f32[8,4,32,128]{3,2,1,0:T(8,128)S(1)} fusion(bf16[128,8,4,32]{0,3,2,1:T(8,128)(2,1)S(1)} %bitcast.102, f32[8,4,128,128]{2,3,1,0:T(8,128)} %get-tuple-element.18, f32[8,4,128]{2,1,0:T(4,128)S(1)} %get-tuple-element.17), kind=kOutput, calls=%fused_computation.25 | convolution fusion | flops 34603008 | bytes 2899968 | tf_op jit(solution)/shard_map/jhik,kjhd->ijhd/dot_general | solution.py:19
  70.6 0.1 fusion.31
  70.8 0.3 fusion.9
  71.1 0.9 %copy.151 = bf16[128,8,128]{2,1,0:T(8,128)(2,1)} copy(bf16[128,8,128]{0,2,1:T(8,128)(2,1)S(1)} %fusion.9) | data formatting | bytes 524288 | tf_op jit(solution)/shard_map/convert_element_type | solution.py:92
  (30 shorter events, 0.3 us)
Async XLA Ops:
  0.0 56.4 %copy-start = (bf16[128,512]{1,0:T(8,128)(2,1)S(1)}, bf16[128,512]{1,0:T(8,128)(2,1)}, u32[]{:S(2)}) copy-start(bf16[128,512]{1,0:T(8,128)(2,1)} %param.12) | copy-start | bytes 393220
  7.4 28.1 %all-to-all-start = ((bf16[16,192,128]{2,1,0:T(8,128)(2,1)}), bf16[16,192,128]{2,1,0:T(8,128)(2,1)S(1)}, u32[]{:S(2)}, u32[]{:S(2)}) async-start(bf16[16,192,128]{2,1,0:T(8,128)(2,1)} %pad_maximum_fusion), calls=%async_computation | async-start | bytes 1572864 | tf_op jit(solution)/shard_map/all_to_all | solution.py:15
  37.3 13.4 %all-to-all-start.1 = ((bf16[16,8,8,128]{3,2,1,0:T(8,128)(2,1)}), bf16[16,8,8,128]{3,2,1,0:T(8,128)(2,1)S(1)}, u32[]{:S(2)}, u32[]{:S(2)}) async-start(bf16[16,8,8,128]{3,2,1,0:T(8,128)(2,1)} %bitcast.92), calls=%async_computation.1 | async-start | bytes 524288 | tf_op jit(solution)/shard_map/all_to_all | solution.py:15
  42.2 1.6 %copy-start.6 = (bf16[128,128]{1,0:T(8,128)(2,1)S(1)}, bf16[128,128]{1,0:T(8,128)(2,1)}, u32[]{:S(2)}) copy-start(bf16[128,128]{1,0:T(8,128)(2,1)} %param.10) | copy-start | bytes 98308
  43.5 7.6 %copy-start.3 = (bf16[128,128]{1,0:T(8,128)(2,1)S(1)}, bf16[128,128]{1,0:T(8,128)(2,1)}, u32[]{:S(2)}) copy-start(bf16[128,128]{1,0:T(8,128)(2,1)} %param.11) | copy-start | bytes 98308
  44.2 7.3 %copy-start.5 = (bf16[128,4]{0,1:T(4,128)(2,1)S(1)}, bf16[128,4]{0,1:T(4,128)(2,1)}, u32[]{:S(2)}) copy-start(bf16[128,4]{0,1:T(4,128)(2,1)} %param.13) | copy-start | bytes 3076
  52.3 12.0 %all-to-all-start.2 = ((bf16[16,4,8,128]{3,2,1,0:T(8,128)(2,1)}), bf16[16,4,8,128]{3,2,1,0:T(8,128)(2,1)}, u32[]{:S(2)}, u32[]{:S(2)}) async-start(bf16[16,4,8,128]{3,2,1,0:T(8,128)(2,1)} %broadcast_in_dim.9), calls=%async_computation.2 | async-start | bytes 262144 | tf_op jit(solution)/shard_map/all_to_all | solution.py:15
  58.0 7.3 %copy-start.1 = (bf16[128,8,128]{0,2,1:T(8,128)(2,1)S(1)}, bf16[128,8,128]{0,2,1:T(8,128)(2,1)}, u32[]{:S(2)}) copy-start(bf16[128,8,128]{0,2,1:T(8,128)(2,1)} %copy.143) | copy-start | bytes 786436
  65.3 3.3 %copy-start.2 = (bf16[128,8,128]{0,2,1:T(8,128)(2,1)S(1)}, bf16[128,8,128]{0,2,1:T(8,128)(2,1)}, u32[]{:S(2)}) copy-start(bf16[128,8,128]{0,2,1:T(8,128)(2,1)} %copy.141) | copy-start | bytes 786436
  68.6 2.2 %copy-start.4 = (bf16[128,128]{1,0:T(8,128)(2,1)S(1)}, bf16[128,128]{1,0:T(8,128)(2,1)}, u32[]{:S(2)}) copy-start(bf16[128,128]{1,0:T(8,128)(2,1)} %param.14) | copy-start | bytes 98308

commit v2 on v1

--- a/solution.py
+++ b/solution.py
@@ -1,7 +1,23 @@
+import functools
+
 import jax
 import jax.numpy as jnp
 from jax import lax
+from jax.experimental import pallas as pl
+from jax.experimental.pallas import tpu as pltpu
 from jax.sharding import PartitionSpec as P
+
+VMEM = pl.BlockSpec(memory_space=pltpu.VMEM)
+SMEM = pl.BlockSpec(memory_space=pltpu.SMEM)
+BF16, F32 = jnp.bfloat16, jnp.float32
+
+
+def dot(a, b, over_a, over_b):
+    return lax.dot_general(a, b, (((over_a,), (over_b,)), ((), ())), preferred_element_type=F32)
+
+
+def sigmoid(x):
+    return 0.5 * jnp.tanh(0.5 * x) + 0.5
 
 
 def layer_norm(x, axis):
@@ -11,15 +27,215 @@
     return centered * lax.rsqrt(spread + 1e-05)
 
 
+def interleave(a, b, blocks):
+    split = (blocks, a.shape[0] // blocks, a.shape[1])
+    return jnp.concatenate([a.reshape(split), b.reshape(split)], axis=1).astype(BF16)
+
+
+def project_kernel(length_ref, pair_ref, w_ref, out_ref):
+    rows, count, channels = pair_ref.shape
+    blocks = out_ref.shape[0]
+    hidden = w_ref.shape[1] // 4
+    first_row = lax.axis_index("dap") * rows
+    length = length_ref[0]
+    key_valid = jnp.where(lax.broadcasted_iota(jnp.int32, (1, count), 1) < length, 1.0, 0.0)
+    w_turned = w_ref[...].T
+    for r in range(rows):
+        x = pair_ref[r].astype(F32)
+        normed = layer_norm(x, 1).astype(BF16)
+        projected = dot(w_turned, normed, 1, 1)
+        mask = key_valid * jnp.where(first_row + r < length, 1.0, 0.0)
+        left = sigmoid(projected[hidden : 2 * hidden]) * projected[:hidden] * mask
+        right = sigmoid(projected[3 * hidden :]) * projected[2 * hidden : 3 * hidden] * mask
+        out_ref[:, 16 * r : 16 * r + 16, :] = interleave(left, right, blocks)
+        if r % 2 == 1:
+            start = 16 * rows + 8 * (r - 1)
+            out_ref[:, start : start + 16, :] = interleave(before, x, blocks)
+        before = x
+
+
+def product_kernel(came_ref, out_ref, wide_ref):
+    blocks, per_block, count = came_ref.shape
+    for p in range(blocks):
+        wide_ref[p * per_block : (p + 1) * per_block, :] = came_ref[p].astype(F32)
+
+    def product(c):
+        left = wide_ref[pl.ds(c, count, stride=16), :].astype(BF16)
+        right = wide_ref[pl.ds(8 + c, count, stride=16), :].astype(BF16)
+        return dot(right, left, 1, 1)
+
+    for c in range(0, 8, 2):
+        out_ref[:, 8 * c : 8 * c + 16, :] = interleave(product(c), product(c + 1), blocks)
+
+
+def gate_kernel(came_ref, w_ref, gate_ref, columns_ref, wide_ref):
+    blocks, per_block, channels = came_ref.shape
+    count, columns = gate_ref.shape[1], gate_ref.shape[0]
+    for p in range(blocks):
+        wide_ref[p * per_block : (p + 1) * per_block, :] = came_ref[p].astype(F32)
+    w = w_ref[...]
+    for j in range(columns):
+        x = wide_ref[pl.ds(j, count, stride=columns), :]
+        columns_ref[j] = x.astype(BF16)
+        gate_ref[j] = sigmoid(dot(layer_norm(x, 1).astype(BF16), w, 1, 0))
+
+
+def middle_kernel(came_ref, gate_ref, columns_ref, w_out_ref, w_bias_ref, bias_ref, normed_ref, mid_ref, wide_ref):
+    columns, count, channels = mid_ref.shape
+    x = came_ref[...].astype(F32).reshape(-1, columns, count)
+    hidden = x.shape[0]
+    wide_ref[...] = layer_norm(x, 0).reshape(hidden * columns, count)
+    w_out = w_out_ref[...]
+    w_bias = w_bias_ref[...]
+    own = lax.broadcasted_iota(jnp.int32, w_bias.shape, 0) % columns
+    total = jnp.zeros((w_bias.shape[0], count), F32)
+    for j in range(columns):
+        product = wide_ref[pl.ds(j, hidden, stride=columns), :].astype(BF16)
+        update = dot(product, w_out, 0, 0)
+        mid = (columns_ref[j].astype(F32) + gate_ref[j] * update).astype(BF16)
+        mid_ref[j] = mid
+        normed = layer_norm(mid.astype(F32), 1).astype(BF16)
+        normed_ref[j] = normed
+        total += dot(jnp.where(own == j, w_bias, 0.0).astype(BF16), normed, 1, 1)
+    bias_ref[...] = jnp.broadcast_to(total.astype(BF16)[None], bias_ref.shape)
+
+
+def heads_kernel(heads, normed_ref, w_ref, q_ref, k_ref, v_ref, g_ref):
+    columns, count, channels = normed_ref.shape
+    width = q_ref.shape[2]
+    size = width // heads
+    w = w_ref[...]
+    w_turned = w[:, 2 * width :].T
+    lane = lax.broadcasted_iota(jnp.int32, (count, width), 1) // size
+    row = lax.broadcasted_iota(jnp.int32, (width, count), 0) // size
+    for j in range(columns):
+        normed = normed_ref[j]
+        qk = dot(normed, w[:, : 2 * width], 1, 0)
+        q_ref[j] = qk[:, :width].astype(BF16)
+        vg = dot(w_turned, normed, 1, 1)
+        g_ref[j] = sigmoid(vg[width:])
+        for h in range(heads):
+            k_ref[j, h * count : (h + 1) * count, :] = jnp.where(lane == h, qk[:, width:], 0.0).astype(BF16)
+            v_ref[j, :, h * count : (h + 1) * count] = jnp.where(row == h, vg[:width], 0.0).astype(BF16)
+
+
+def attention_kernel(heads, length_ref, bias_ref, q_ref, k_ref, v_ref, g_ref, mid_ref, w_ref, out_ref, wide_ref):
+    columns, count, width = q_ref.shape
+    size = width // heads
+    blocks = bias_ref.shape[0]
+    invalid = lax.broadcasted_iota(jnp.int32, (count, count), 0) >= length_ref[0]
+    arrived = bias_ref[...].astype(F32).reshape(blocks, heads, columns, count)
+    bias = [arrived[:, h].reshape(count, count).T for h in range(heads)]
+    w = w_ref[...]
+    for j in range(columns):
+        q = q_ref[j]
+        parts = []
+        for h in range(heads):
+            score = dot(k_ref[j, h * count : (h + 1) * count, :], q, 1, 1) * size ** (-0.5) + bias[h]
+            score = jnp.where(invalid, -1000000000.0, score)
+            expo = jnp.exp(score - jnp.max(score, axis=0, keepdims=True))
+            total = jnp.sum(expo, axis=0, keepdims=True)
+            parts.append((expo * (1.0 / total)).astype(BF16))
+        output = dot(v_ref[j], jnp.concatenate(parts, axis=0), 1, 0)
+        attended = (g_ref[j] * output).astype(BF16)
+        result = dot(attended, w, 0, 0) + mid_ref[j].astype(F32)
+        wide_ref[pl.ds(j, count, stride=columns), :] = result
+    out_ref[...] = wide_ref[...].reshape(count, columns, w.shape[1]).astype(BF16)
+
+
+def call(kernel, outs, operands, specs=None, scratch=(), flops=0, grid=()):
+    size = sum(a.size * a.dtype.itemsize for a in list(operands) + list(outs))
+    return pl.pallas_call(
+        kernel,
+        grid=grid,
+        out_shape=[jax.ShapeDtypeStruct(o.shape, o.dtype) for o in outs],
+        in_specs=[VMEM] * len(operands) if specs is None else specs,
+        out_specs=[VMEM] * len(outs),
+        scratch_shapes=list(scratch),
+        cost_estimate=pl.CostEstimate(flops=flops, bytes_accessed=size, transcendentals=0),
+        compiler_params=pltpu.CompilerParams(vmem_limit_bytes=24 * 2**20),
+    )(*operands)
+
+
+def shape(dims, dtype):
+    return jax.ShapeDtypeStruct(dims, dtype)
+
+
 def exchange(x):
     return lax.all_to_all(x, "dap", split_axis=0, concat_axis=0, tiled=True)
 
 
+def kernel_body(pair, w_proj, w_gate_out, w_out, w_qkvg, w_bias, w_att_out, length):
+    rows, count, channels = pair.shape
+    hidden = w_out.shape[0]
+    blocks = count // rows
+    heads, width = w_bias.shape[1], w_att_out.shape[0]
+    square = (rows, count, channels)
+    wide = pltpu.VMEM((rows * count, channels), F32)
+
+    (sent,) = call(
+        project_kernel,
+        [shape((blocks, 24 * rows, count), BF16)],
+        (length, pair, w_proj),
+        [SMEM, VMEM, VMEM],
+        flops=2 * pair.size * 4 * hidden,
+    )
+    came = exchange(sent)
+    (product,) = call(
+        product_kernel,
+        [shape((blocks, 8 * rows, count), BF16)],
+        (came,),
+        [pl.BlockSpec((blocks, 16 * rows, count), lambda _: (0, 0, 0))],
+        [pltpu.VMEM((blocks * 16 * rows, count), F32)],
+        flops=2 * 8 * count**3,
+        grid=(1,),
+    )
+    arrived = exchange(product)
+    gate, columns = call(
+        gate_kernel,
+        [shape(square, F32), shape(square, BF16)],
+        (came, w_gate_out),
+        [pl.BlockSpec((blocks, 8 * rows, channels), lambda _: (0, 2, 0)), VMEM],
+        [wide],
+        flops=2 * pair.size * channels,
+        grid=(1,),
+    )
+    w_rows = jnp.repeat(w_bias.T, rows, axis=0).astype(F32)
+    bias, normed, mid = call(
+        middle_kernel,
+        [shape((blocks, heads * rows, count), BF16), shape(square, BF16), shape(square, BF16)],
+        (arrived, gate, columns, w_out, w_rows),
+        scratch=[wide],
+        flops=2 * pair.size * channels,
+    )
+    bias = exchange(bias)
+    q, k, v, g = call(
+        functools.partial(heads_kernel, heads),
+        [
+            shape((rows, count, width), BF16),
+            shape((rows, heads * count, width), BF16),
+            shape((rows, width, heads * count), BF16),
+            shape((rows, width, count), F32),
+        ],
+        (normed, w_qkvg),
+        flops=2 * pair.size * 4 * width,
+    )
+    (out,) = call(
+        functools.partial(attention_kernel, heads),
+        [shape((count, rows, channels), BF16)],
+        (length, bias, q, k, v, g, mid, w_att_out),
+        [SMEM] + [VMEM] * 7,
+        [wide],
+        flops=2 * pair.size * count * 8,
+    )
+    return out
+
+
 def matmul(spec, a, b):
     return jnp.einsum(spec, a, b, preferred_element_type=jnp.float32)
 
 
-def body(pair, w_proj, w_gate_out, w_out, w_qkvg, w_bias, w_att_out, length):
+def whole_body(pair, w_proj, w_gate_out, w_out, w_qkvg, w_bias, w_att_out, length):
     row_count, full_count, channels = pair.shape
     hidden = w_out.shape[0]
     device_count = full_count // row_count
@@ -92,6 +308,14 @@
     return result.astype(jnp.bfloat16)
 
 
+def body(pair, w_proj, w_gate_out, w_out, w_qkvg, w_bias, w_att_out, length):
+    rows, count, channels = pair.shape
+    share = w_out.shape[0] * rows // count
+    fits = share == rows == 8 and count == channels == w_att_out.shape[0] == 128
+    chosen = kernel_body if fits else whole_body
+    return chosen(pair, w_proj, w_gate_out, w_out, w_qkvg, w_bias, w_att_out, length)
+
+
 def solution(mesh):
     placed = (P(("rep", "dap"), None, None), P(), P(), P(), P(), P(), P(), P("rep"))
     return jax.shard_map(

time: 72.5 us -> 65.7 us (0.906)
  blocking collectives: 0 us -> 29.4 us
  waiting for transfers between devices: 30.5 us -> 14.8 us
  starting transfers between devices: 17.4 us -> 7.34 us
  Pallas kernels: 0 us -> 10 us
  matrix products: 8.58 us -> 0 us
  other arithmetic: 6.27 us -> 0.01 us
  local copies, waits for them, and re-layouts: 8.24 us -> 2.82 us
    all_to_all x0 -> x1, blocking collectives: none -> 29.4 us  [exchange(): return lax.all_to_all(x, 'dap', split_axis=0, concat_axis=0, tiled=True)]
    all_to_all x3 -> x2, waiting for transfers between devices: 30.5 us -> 14.8 us  [exchange(): return lax.all_to_all(x, 'dap', split_axis=0, concat_axis=0, tiled=True)]
    all_to_all x3 -> x2, starting transfers between devices: 17.4 us -> 7.34 us  [exchange(): return lax.all_to_all(x, 'dap', split_axis=0, concat_axis=0, tiled=True)]
    pallas_call x0 -> x6, Pallas kernels: none -> 10 us  [call(): pl.pallas_call(kernel, grid=grid, out_shape=[jax.ShapeDtypeStruct(o.shape...]
    dot_general x8 -> x0, matrix products: 5.28 us -> none  [matmul(): return jnp.einsum(spec, a, b, preferred_element_type=jnp.float32)]
    reduce_sum x7 -> x0, other arithmetic: 3.36 us -> none  [the longest x4 1.89 us: layer_norm(): spread = jnp.mean(centered * centered, axis=axis, keepdims=True)]
    sub x1 -> x0, matrix products: 3.3 us -> none  [body(): expo = jnp.exp(score - top)]
    slice x5 -> x0, local copies, waits for them, and re-layouts: 2.84 us -> none  [the longest x2 1.05 us: body(): keys = mixed[..., width:2 * width].astype(jnp.bfloat16).reshape(per_head)]
  transfers between devices with their start and end apart: 3 -> 2, of which waited for: 3 -> 2; matrix products, arithmetic and copies ran while one was open for 8% -> 0% of each run, Pallas kernels for 0% -> 2%
where the time goes in v2:
time: 65.7 us; the launch traced here: 65.2 us
  blocking collectives  29.4 us (45%)
  waiting for transfers between devices  14.8 us (23%)
  Pallas kernels  10 us (15%)
  starting transfers between devices  7.34 us (11%)
  local copies, waits for them, and re-layouts  2.82 us (4%)
  between operations  0.77 us (1%)
    all_to_all x1, blocking collectives, exchange(): return lax.all_to_all(x, 'dap', split_axis=0, concat_axis=0, tiled=True)  29.4 us
    all_to_all x2, waiting for transfers between devices, exchange(): return lax.all_to_all(x, 'dap', split_axis=0, concat_axis=0, tiled=True)  14.8 us
    pallas_call x6, Pallas kernels, call(): pl.pallas_call(kernel, grid=grid, out_shape=[jax.ShapeDtypeStruct(o.shape...  10 us
    all_to_all x2, starting transfers between devices, exchange(): return lax.all_to_all(x, 'dap', split_axis=0, concat_axis=0, tiled=True)  7.34 us
    unnamed x18, local copies, waits for them, and re-layouts  2.82 us
  transfers between devices with their start and end apart: 2, of which 2 were waited for; matrix products, arithmetic and copies ran while one was open for 0% of the time, Pallas kernels for 2%

profile of v2, /device:TPU:0, one launch (start us, length us, event | category | flops | bytes accessed | tf_op | source)
XLA Modules:
  0.0 65.2 jit_solution(14679794331582924420)
XLA Ops:
  0.7 0.0 copy-start
  0.7 0.9 %copy-done = bf16[8,128,128]{2,1,0:T(8,128)(2,1)S(1)} copy-done((bf16[8,128,128]{2,1,0:T(8,128)(2,1)S(1)}, bf16[8,128,128]{2,1,0:T(8,128)(2,1)}, u32[]{:S(2)}) %copy-start) | copy-done | bytes 262168
  1.6 0.0 copy-start.1
  1.6 0.9 %copy-done.1 = bf16[128,512]{1,0:T(8,128)(2,1)S(1)} copy-done((bf16[128,512]{1,0:T(8,128)(2,1)S(1)}, bf16[128,512]{1,0:T(8,128)(2,1)}, u32[]{:S(2)}) %copy-start.1) | copy-done | bytes 131096
  2.5 0.9 %shard_map.82 = bf16[16,192,128]{2,1,0:T(8,128)(2,1)S(1)} custom-call(s32[1]{0:T(128)S(6)} %copy.9.length_ref, bf16[8,128,128]{2,1,0:T(8,128)(2,1)S(1)} %copy-done, bf16[128,512]{1,0:T(8,128)(2,1)S(1)} %copy-done.1), custom_call_target="tpu_custom_call" | custom-call | flops 134217728 | bytes 1179652 | tf_op jit(solution)/shard_map/pallas_call | solution.py:148
  3.5 29.4 %all_to_all.15.came_ref = bf16[16,192,128]{2,1,0:T(8,128)(2,1)S(1)} all-to-all(bf16[16,192,128]{2,1,0:T(8,128)(2,1)S(1)} %shard_map.82), channel_id=1, replica_groups=mesh['dap'=16,'rep'=2] {'dap'}, dimensions={0} | all-to-all | bytes 1572864 | tf_op jit(solution)/shard_map/all_to_all | solution.py:165
  32.8 1.2 %shard_map.83 = bf16[16,64,128]{2,1,0:T(8,128)(2,1)} custom-call(bf16[16,192,128]{2,1,0:T(8,128)(2,1)S(1)} %all_to_all.15.came_ref), custom_call_target="tpu_custom_call" | custom-call | flops 33554432 | bytes 1048576 | tf_op jit(solution)/shard_map/pallas_call | solution.py:148
  34.1 0.0 copy-start.8
  34.1 0.0 copy-start.3
  34.1 3.7 %all-to-all-start.1 = ((bf16[16,64,128]{2,1,0:T(8,128)(2,1)}), bf16[16,64,128]{2,1,0:T(8,128)(2,1)S(1)}, u32[]{:S(2)}, u32[]{:S(2)}) async-start(bf16[16,64,128]{2,1,0:T(8,128)(2,1)} %shard_map.83), calls=%async_computation.1 | async-start | bytes 524288 | tf_op jit(solution)/shard_map/all_to_all | solution.py:165
  37.7 0.0 copy-done.8
  37.8 0.0 copy-done.3
  37.8 0.0 copy-start.4
  37.8 0.5 shard_map.84
  38.3 8.5 %all-to-all-done.1.came_ref = bf16[16,64,128]{2,1,0:T(8,128)(2,1)S(1)} async-done(((bf16[16,64,128]{2,1,0:T(8,128)(2,1)}), bf16[16,64,128]{2,1,0:T(8,128)(2,1)S(1)}, u32[]{:S(2)}, u32[]{:S(2)}) %all-to-all-start.1) | async-done | bytes 262176 | tf_op jit(solution)/shard_map/all_to_all | solution.py:165
  46.9 0.0 copy-done.4
  46.9 2.2 %shard_map.85 = (bf16[16,32,128]{2,1,0:T(8,128)(2,1)}, bf16[8,128,128]{2,1,0:T(8,128)(2,1)S(1)}, bf16[8,128,128]{2,1,0:T(8,128)(2,1)S(1)}) custom-call(bf16[16,64,128]{2,1,0:T(8,128)(2,1)S(1)} %all-to-all-done.1.came_ref, f32[8,128,128]{2,1,0:T(8,128)S(1)} %get-tuple-element.14.gate_ref, bf16[8,128,128]{2,1,0:T(8,128)(2,1)S(1)} %get-tuple-element.15.columns_ref, ...), custom_call_target="tpu_custom_call" | custom-call | flops 33554432 | bytes 1753088 | tf_op jit(solution)/shard_map/pallas_call | solution.py:148
  49.1 0.0 copy-start.5
  49.1 0.0 copy-start.7
  49.1 3.7 %all-to-all-start.2 = ((bf16[16,32,128]{2,1,0:T(8,128)(2,1)}), bf16[16,32,128]{2,1,0:T(8,128)(2,1)S(1)}, u32[]{:S(2)}, u32[]{:S(2)}) async-start(bf16[16,32,128]{2,1,0:T(8,128)(2,1)} %get-tuple-element.16), calls=%async_computation.2 | async-start | bytes 262144 | tf_op jit(solution)/shard_map/all_to_all | solution.py:165
  52.8 0.0 copy-done.5
  52.8 0.0 copy-done.7
  52.8 0.0 copy-start.6
  52.8 0.9 %copy-done.6 = bf16[8,128,128]{2,1,0:T(8,128)(2,1)S(1)} copy-done((bf16[8,128,128]{2,1,0:T(8,128)(2,1)S(1)}, bf16[8,128,128]{2,1,0:T(8,128)(2,1)}, u32[]{:S(2)}) %copy-start.6) | copy-done | bytes 262168
  53.8 0.0 copy-start.2
  53.8 0.5 shard_map.86
  54.3 6.3 %all-to-all-done.2.bias_ref = bf16[16,32,128]{2,1,0:T(8,128)(2,1)S(1)} async-done(((bf16[16,32,128]{2,1,0:T(8,128)(2,1)}), bf16[16,32,128]{2,1,0:T(8,128)(2,1)S(1)}, u32[]{:S(2)}, u32[]{:S(2)}) %all-to-all-start.2) | async-done | bytes 131104 | tf_op jit(solution)/shard_map/all_to_all | solution.py:165
  60.6 0.0 copy-done.2
  60.6 4.6 %shard_map.87 = bf16[128,8,128]{2,1,0:T(8,128)(2,1)} custom-call(s32[1]{0:T(128)S(6)} %copy.9.length_ref, bf16[16,32,128]{2,1,0:T(8,128)(2,1)S(1)} %all-to-all-done.2.bias_ref, bf16[8,128,128]{2,1,0:T(8,128)(2,1)S(1)} %get-tuple-element.18.q_ref, bf16[8,512,128]{2,1,0:T(8,128)(2,1)S(1)} %get-tuple-element.19.k_ref, ...), custom_call_target="tpu_custom_call" | custom-call | flops 268435456 | bytes 3571716 | tf_op jit(solution)/shard_map/pallas_call | solution.py:148
  (2 shorter events, 0.0 us)
Async XLA Ops:
  0.7 1.0 %copy-start = (bf16[8,128,128]{2,1,0:T(8,128)(2,1)S(1)}, bf16[8,128,128]{2,1,0:T(8,128)(2,1)}, u32[]{:S(2)}) copy-start(bf16[8,128,128]{2,1,0:T(8,128)(2,1)} %pair_ref.1) | copy-start | bytes 786436
  1.6 0.9 %copy-start.1 = (bf16[128,512]{1,0:T(8,128)(2,1)S(1)}, bf16[128,512]{1,0:T(8,128)(2,1)}, u32[]{:S(2)}) copy-start(bf16[128,512]{1,0:T(8,128)(2,1)} %w_ref.4) | copy-start | bytes 393220
  34.1 3.7 %copy-start.8 = (bf16[128,4]{0,1:T(4,128)(2,1)S(1)}, bf16[128,4]{0,1:T(4,128)(2,1)}, u32[]{:S(2)}) copy-start(bf16[128,4]{0,1:T(4,128)(2,1)} %param.13) | copy-start | bytes 3076
  34.1 3.7 %copy-start.3 = (bf16[128,128]{1,0:T(8,128)(2,1)S(1)}, bf16[128,128]{1,0:T(8,128)(2,1)}, u32[]{:S(2)}) copy-start(bf16[128,128]{1,0:T(8,128)(2,1)} %w_ref.5) | copy-start | bytes 98308
  34.1 12.8 %all-to-all-start.1 = ((bf16[16,64,128]{2,1,0:T(8,128)(2,1)}), bf16[16,64,128]{2,1,0:T(8,128)(2,1)S(1)}, u32[]{:S(2)}, u32[]{:S(2)}) async-start(bf16[16,64,128]{2,1,0:T(8,128)(2,1)} %shard_map.83), calls=%async_computation.1 | async-start | bytes 524288 | tf_op jit(solution)/shard_map/all_to_all | solution.py:165
  37.8 9.1 %copy-start.4 = (bf16[128,128]{1,0:T(8,128)(2,1)S(1)}, bf16[128,128]{1,0:T(8,128)(2,1)}, u32[]{:S(2)}) copy-start(bf16[128,128]{1,0:T(8,128)(2,1)} %w_out_ref.1) | copy-start | bytes 98308
  49.1 3.7 %copy-start.5 = (bf16[8,128,128]{2,1,0:T(8,128)(2,1)}, bf16[8,128,128]{2,1,0:T(8,128)(2,1)S(1)}, u32[]{:S(2)}) copy-start(bf16[8,128,128]{2,1,0:T(8,128)(2,1)S(1)} %get-tuple-element.17.normed_ref) | copy-start | bytes 786436
  49.1 3.7 %copy-start.7 = (bf16[128,512]{1,0:T(8,128)(2,1)S(1)}, bf16[128,512]{1,0:T(8,128)(2,1)}, u32[]{:S(2)}) copy-start(bf16[128,512]{1,0:T(8,128)(2,1)} %w_ref.6) | copy-start | bytes 393220
  49.1 11.5 %all-to-all-start.2 = ((bf16[16,32,128]{2,1,0:T(8,128)(2,1)}), bf16[16,32,128]{2,1,0:T(8,128)(2,1)S(1)}, u32[]{:S(2)}, u32[]{:S(2)}) async-start(bf16[16,32,128]{2,1,0:T(8,128)(2,1)} %get-tuple-element.16), calls=%async_computation.2 | async-start | bytes 262144 | tf_op jit(solution)/shard_map/all_to_all | solution.py:165
  52.8 1.0 %copy-start.6 = (bf16[8,128,128]{2,1,0:T(8,128)(2,1)S(1)}, bf16[8,128,128]{2,1,0:T(8,128)(2,1)}, u32[]{:S(2)}) copy-start(bf16[8,128,128]{2,1,0:T(8,128)(2,1)} %copy-done.5) | copy-start | bytes 786436
  53.8 6.8 %copy-start.2 = (bf16[128,128]{1,0:T(8,128)(2,1)S(1)}, bf16[128,128]{1,0:T(8,128)(2,1)}, u32[]{:S(2)}) copy-start(bf16[128,128]{1,0:T(8,128)(2,1)} %w_ref.7) | copy-start | bytes 98308

commit v3 on v2

--- a/solution.py
+++ b/solution.py
@@ -9,7 +9,9 @@
 
 VMEM = pl.BlockSpec(memory_space=pltpu.VMEM)
 SMEM = pl.BlockSpec(memory_space=pltpu.SMEM)
+HBM = pl.BlockSpec(memory_space=pltpu.HBM)
 BF16, F32 = jnp.bfloat16, jnp.float32
+LOG2E = 1.4426950408889634
 
 
 def dot(a, b, over_a, over_b):
@@ -32,15 +34,24 @@
     return jnp.concatenate([a.reshape(split), b.reshape(split)], axis=1).astype(BF16)
 
 
-def project_kernel(length_ref, pair_ref, w_ref, out_ref):
+def project_kernel(length_ref, pair_hbm, w_hbm, out_ref, pair_ref, w_ref, sems):
     rows, count, channels = pair_ref.shape
     blocks = out_ref.shape[0]
     hidden = w_ref.shape[1] // 4
+    copies = [pltpu.make_async_copy(w_hbm, w_ref, sems.at[0])]
+    for r in range(0, rows, 2):
+        part = pl.ds(r, 2)
+        copies.append(pltpu.make_async_copy(pair_hbm.at[part], pair_ref.at[part], sems.at[1 + r // 2]))
+    for copy in copies:
+        copy.start()
     first_row = lax.axis_index("dap") * rows
     length = length_ref[0]
     key_valid = jnp.where(lax.broadcasted_iota(jnp.int32, (1, count), 1) < length, 1.0, 0.0)
+    copies[0].wait()
     w_turned = w_ref[...].T
     for r in range(rows):
+        if r % 2 == 0:
+            copies[1 + r // 2].wait()
         x = pair_ref[r].astype(F32)
         normed = layer_norm(x, 1).astype(BF16)
         projected = dot(w_turned, normed, 1, 1)
@@ -55,9 +66,9 @@
 
 
 def product_kernel(came_ref, out_ref, wide_ref):
-    blocks, per_block, count = came_ref.shape
-    for p in range(blocks):
-        wide_ref[p * per_block : (p + 1) * per_block, :] = came_ref[p].astype(F32)
+    blocks, per_block, count = out_ref.shape[0], 2 * out_ref.shape[1], out_ref.shape[2]
+    for p in range(blocks):
+        wide_ref[p * per_block : (p + 1) * per_block, :] = came_ref[p, :per_block].astype(F32)
 
     def product(c):
         left = wide_ref[pl.ds(c, count, stride=16), :].astype(BF16)
@@ -69,10 +80,10 @@
 
 
 def gate_kernel(came_ref, w_ref, gate_ref, columns_ref, wide_ref):
-    blocks, per_block, channels = came_ref.shape
-    count, columns = gate_ref.shape[1], gate_ref.shape[0]
-    for p in range(blocks):
-        wide_ref[p * per_block : (p + 1) * per_block, :] = came_ref[p].astype(F32)
+    columns, count = gate_ref.shape[0], gate_ref.shape[1]
+    blocks, per_block = came_ref.shape[0], columns * columns
+    for p in range(blocks):
+        wide_ref[p * per_block : (p + 1) * per_block, :] = came_ref[p, 2 * per_block :].astype(F32)
     w = w_ref[...]
     for j in range(columns):
         x = wide_ref[pl.ds(j, count, stride=columns), :]
@@ -82,72 +93,102 @@
 
 def middle_kernel(came_ref, gate_ref, columns_ref, w_out_ref, w_bias_ref, bias_ref, normed_ref, mid_ref, wide_ref):
     columns, count, channels = mid_ref.shape
-    x = came_ref[...].astype(F32).reshape(-1, columns, count)
-    hidden = x.shape[0]
-    wide_ref[...] = layer_norm(x, 0).reshape(hidden * columns, count)
+    blocks, per_block, _ = came_ref.shape
+    hidden = blocks * per_block // columns
+
+    def load(p):
+        return came_ref[p].astype(F32).reshape(per_block // columns, columns, count)
+
+    mean = jnp.zeros((columns, count), F32)
+    for p in range(blocks):
+        mean += jnp.sum(load(p), axis=0)
+    mean = mean * (1.0 / hidden)
+    spread = jnp.zeros((columns, count), F32)
+    for p in range(blocks):
+        spread += jnp.sum(jnp.square(load(p) - mean), axis=0)
+    scale = lax.rsqrt(spread * (1.0 / hidden) + 1e-05)
+    for p in range(blocks):
+        part = (load(p) - mean) * scale
+        wide_ref[p * per_block : (p + 1) * per_block, :] = part.reshape(per_block, count)
     w_out = w_out_ref[...]
+    for j in range(columns):
+        product = wide_ref[pl.ds(j, hidden, stride=columns), :].astype(BF16)
+        update = dot(product, w_out, 0, 0)
+        mid_ref[j] = (columns_ref[j].astype(F32) + gate_ref[j] * update).astype(BF16)
+    for j in range(columns):
+        normed_ref[j] = layer_norm(mid_ref[j].astype(F32), 1).astype(BF16)
     w_bias = w_bias_ref[...]
     own = lax.broadcasted_iota(jnp.int32, w_bias.shape, 0) % columns
     total = jnp.zeros((w_bias.shape[0], count), F32)
     for j in range(columns):
-        product = wide_ref[pl.ds(j, hidden, stride=columns), :].astype(BF16)
-        update = dot(product, w_out, 0, 0)
-        mid = (columns_ref[j].astype(F32) + gate_ref[j] * update).astype(BF16)
-        mid_ref[j] = mid
-        normed = layer_norm(mid.astype(F32), 1).astype(BF16)
-        normed_ref[j] = normed
-        total += dot(jnp.where(own == j, w_bias, 0.0).astype(BF16), normed, 1, 1)
+        total += dot(jnp.where(own == j, w_bias, 0.0).astype(BF16), normed_ref[j], 1, 1)
     bias_ref[...] = jnp.broadcast_to(total.astype(BF16)[None], bias_ref.shape)
 
 
-def heads_kernel(heads, normed_ref, w_ref, q_ref, k_ref, v_ref, g_ref):
+def heads_kernel(heads, length_ref, normed_ref, w_ref, score_ref, v_ref, gate_ref):
     columns, count, channels = normed_ref.shape
-    width = q_ref.shape[2]
+    width = gate_ref.shape[1]
     size = width // heads
     w = w_ref[...]
     w_turned = w[:, 2 * width :].T
     lane = lax.broadcasted_iota(jnp.int32, (count, width), 1) // size
     row = lax.broadcasted_iota(jnp.int32, (width, count), 0) // size
+    valid = lax.broadcasted_iota(jnp.int32, (count, count), 0) < length_ref[0]
+    extra = (v_ref.shape[1] - width, heads * count)
+    extra_head = lax.broadcasted_iota(jnp.int32, extra, 1) // count
+    ones = jnp.where(lax.broadcasted_iota(jnp.int32, extra, 0) == extra_head, 1.0, 0.0).astype(BF16)
     for j in range(columns):
         normed = normed_ref[j]
         qk = dot(normed, w[:, : 2 * width], 1, 0)
-        q_ref[j] = qk[:, :width].astype(BF16)
+        q = qk[:, :width].astype(BF16)
         vg = dot(w_turned, normed, 1, 1)
-        g_ref[j] = sigmoid(vg[width:])
+        gate_ref[j] = sigmoid(vg[width:])
+        v_ref[j, width:, :] = ones
         for h in range(heads):
-            k_ref[j, h * count : (h + 1) * count, :] = jnp.where(lane == h, qk[:, width:], 0.0).astype(BF16)
-            v_ref[j, :, h * count : (h + 1) * count] = jnp.where(row == h, vg[:width], 0.0).astype(BF16)
-
-
-def attention_kernel(heads, length_ref, bias_ref, q_ref, k_ref, v_ref, g_ref, mid_ref, w_ref, out_ref, wide_ref):
-    columns, count, width = q_ref.shape
+            own = slice(h * count, (h + 1) * count)
+            k = jnp.where(lane == h, qk[:, width:], 0.0).astype(BF16)
+            score = dot(k, q, 1, 1) * (size ** (-0.5) * LOG2E)
+            score_ref[j, own, :] = jnp.where(valid, score, 0.0)
+            v_ref[j, :width, own] = jnp.where(row == h, vg[:width], 0.0).astype(BF16)
+
+
+def attention_kernel(
+    heads, length_ref, bias_ref, score_ref, v_ref, gate_ref, mid_ref, w_ref, out_ref, wide_ref, expo_ref, attended_ref
+):
+    columns, width, count = gate_ref.shape
     size = width // heads
     blocks = bias_ref.shape[0]
     invalid = lax.broadcasted_iota(jnp.int32, (count, count), 0) >= length_ref[0]
     arrived = bias_ref[...].astype(F32).reshape(blocks, heads, columns, count)
-    bias = [arrived[:, h].reshape(count, count).T for h in range(heads)]
+    for h in range(heads):
+        own = slice(h * count, (h + 1) * count)
+        bias = arrived[:, h].reshape(count, count).T * LOG2E
+        bias = jnp.where(invalid, -1000000000.0 * LOG2E, bias)
+        tops = []
+        for j in range(columns):
+            score = score_ref[j, own, :] + bias
+            tops.append(jnp.max(score.reshape(-1, 8, count), axis=0))
+        tops = [jnp.max(top, axis=0, keepdims=True) for top in tops]
+        for j in range(columns):
+            expo_ref[j, own, :] = jnp.exp2(score_ref[j, own, :] + bias - tops[j]).astype(BF16)
+    for j in range(columns):
+        output = dot(v_ref[j], expo_ref[j], 1, 0)
+        scale = 1.0 / output[width : width + heads]
+        for h in range(heads):
+            own = slice(h * size, (h + 1) * size)
+            attended = gate_ref[j, own, :] * (output[own] * scale[h : h + 1])
+            attended_ref[j, own, :] = attended.astype(BF16)
     w = w_ref[...]
     for j in range(columns):
-        q = q_ref[j]
-        parts = []
-        for h in range(heads):
-            score = dot(k_ref[j, h * count : (h + 1) * count, :], q, 1, 1) * size ** (-0.5) + bias[h]
-            score = jnp.where(invalid, -1000000000.0, score)
-            expo = jnp.exp(score - jnp.max(score, axis=0, keepdims=True))
-            total = jnp.sum(expo, axis=0, keepdims=True)
-            parts.append((expo * (1.0 / total)).astype(BF16))
-        output = dot(v_ref[j], jnp.concatenate(parts, axis=0), 1, 0)
-        attended = (g_ref[j] * output).astype(BF16)
-        result = dot(attended, w, 0, 0) + mid_ref[j].astype(F32)
+        result = dot(attended_ref[j], w, 0, 0) + mid_ref[j].astype(F32)
         wide_ref[pl.ds(j, count, stride=columns), :] = result
     out_ref[...] = wide_ref[...].reshape(count, columns, w.shape[1]).astype(BF16)
 
 
-def call(kernel, outs, operands, specs=None, scratch=(), flops=0, grid=()):
+def call(kernel, outs, operands, specs=None, scratch=(), flops=0):
     size = sum(a.size * a.dtype.itemsize for a in list(operands) + list(outs))
     return pl.pallas_call(
         kernel,
-        grid=grid,
         out_shape=[jax.ShapeDtypeStruct(o.shape, o.dtype) for o in outs],
         in_specs=[VMEM] * len(operands) if specs is None else specs,
         out_specs=[VMEM] * len(outs),
@@ -177,7 +218,12 @@
         project_kernel,
         [shape((blocks, 24 * rows, count), BF16)],
         (length, pair, w_proj),
-        [SMEM, VMEM, VMEM],
+        [SMEM, HBM, HBM],
+        [
+            pltpu.VMEM(pair.shape, BF16),
+            pltpu.VMEM(w_proj.shape, BF16),
+            pltpu.SemaphoreType.DMA((1 + rows // 2,)),
+        ],
         flops=2 * pair.size * 4 * hidden,
     )
     came = exchange(sent)
@@ -185,20 +231,16 @@
         product_kernel,
         [shape((blocks, 8 * rows, count), BF16)],
         (came,),
-        [pl.BlockSpec((blocks, 16 * rows, count), lambda _: (0, 0, 0))],
-        [pltpu.VMEM((blocks * 16 * rows, count), F32)],
+        scratch=[pltpu.VMEM((blocks * 16 * rows, count), F32)],
         flops=2 * 8 * count**3,
-        grid=(1,),
     )
     arrived = exchange(product)
     gate, columns = call(
         gate_kernel,
         [shape(square, F32), shape(square, BF16)],
         (came, w_gate_out),
-        [pl.BlockSpec((blocks, 8 * rows, channels), lambda _: (0, 2, 0)), VMEM],
-        [wide],
+        scratch=[wide],
         flops=2 * pair.size * channels,
-        grid=(1,),
     )
     w_rows = jnp.repeat(w_bias.T, rows, axis=0).astype(F32)
     bias, normed, mid = call(
@@ -209,23 +251,23 @@
         flops=2 * pair.size * channels,
     )
     bias = exchange(bias)
-    q, k, v, g = call(
+    score, v, gate = call(
         functools.partial(heads_kernel, heads),
         [
-            shape((rows, count, width), BF16),
-            shape((rows, heads * count, width), BF16),
-            shape((rows, width, heads * count), BF16),
+            shape((rows, heads * count, count), F32),
+            shape((rows, width + 16, heads * count), BF16),
             shape((rows, width, count), F32),
         ],
-        (normed, w_qkvg),
-        flops=2 * pair.size * 4 * width,
+        (length, normed, w_qkvg),
+        [SMEM, VMEM, VMEM],
+        flops=2 * pair.size * 8 * width,
     )
     (out,) = call(
         functools.partial(attention_kernel, heads),
         [shape((count, rows, channels), BF16)],
-        (length, bias, q, k, v, g, mid, w_att_out),
-        [SMEM] + [VMEM] * 7,
-        [wide],
+        (length, bias, score, v, gate, mid, w_att_out),
+        [SMEM] + [VMEM] * 6,
+        [wide, pltpu.VMEM((rows, heads * count, count), BF16), pltpu.VMEM((rows, width, count), BF16)],
         flops=2 * pair.size * count * 8,
     )
     return out

time: 65.7 us -> 67 us (1.020)
  local copies, waits for them, and re-layouts: 2.82 us -> 7.9 us
  waiting for transfers between devices: 14.8 us -> 11.8 us
    unnamed x18 -> x26, local copies, waits for them, and re-layouts: 2.82 us -> 7.89 us
    all_to_all x2, waiting for transfers between devices: 14.8 us -> 11.8 us  [exchange(): return lax.all_to_all(x, 'dap', split_axis=0, concat_axis=0, tiled=True)]
  transfers between devices with their start and end apart: 2 -> 2, of which waited for: 2 -> 2; matrix products, arithmetic and copies ran while one was open for 0% -> 0% of each run, Pallas kernels for 2% -> 4%
where the time goes in v3:
time: 67 us; the launch traced here: 66.4 us
  blocking collectives  29.4 us (44%)
  waiting for transfers between devices  11.8 us (18%)
  Pallas kernels  9.36 us (14%)
  local copies, waits for them, and re-layouts  7.9 us (12%)
  starting transfers between devices  7.2 us (11%)
  between operations  0.77 us (1%)
    all_to_all x1, blocking collectives, exchange(): return lax.all_to_all(x, 'dap', split_axis=0, concat_axis=0, tiled=True)  29.4 us
    all_to_all x2, waiting for transfers between devices, exchange(): return lax.all_to_all(x, 'dap', split_axis=0, concat_axis=0, tiled=True)  11.8 us
    pallas_call x6, Pallas kernels, call(): pl.pallas_call(kernel, out_shape=[jax.ShapeDtypeStruct(o.shape, o.dtype)...  9.36 us
    unnamed x26, local copies, waits for them, and re-layouts  7.89 us
    all_to_all x2, starting transfers between devices, exchange(): return lax.all_to_all(x, 'dap', split_axis=0, concat_axis=0, tiled=True)  7.2 us
  transfers between devices with their start and end apart: 2, of which 2 were waited for; matrix products, arithmetic and copies ran while one was open for 0% of the time, Pallas kernels for 4%

profile of v3, /device:TPU:0, one launch (start us, length us, event | category | flops | bytes accessed | tf_op | source)
XLA Modules:
  0.0 66.4 jit_solution(15631763166120336020)
XLA Ops:
  0.7 0.0 copy-start.4
  0.7 0.9 %copy-done.4 = bf16[8,128,128]{2,1,0:T(8,128)(2,1)S(1)} copy-done((bf16[8,128,128]{2,1,0:T(8,128)(2,1)S(1)}, bf16[8,128,128]{2,1,0:T(8,128)(2,1)}, u32[]{:S(2)}) %copy-start.4) | copy-done | bytes 262168
  1.6 0.0 copy-start.5
  1.6 0.9 %copy-done.5 = bf16[128,512]{1,0:T(8,128)(2,1)S(1)} copy-done((bf16[128,512]{1,0:T(8,128)(2,1)S(1)}, bf16[128,512]{1,0:T(8,128)(2,1)}, u32[]{:S(2)}) %copy-start.5) | copy-done | bytes 131096
  2.5 0.0 copy-start.12
  2.5 0.0 copy-start.7
  2.5 2.3 %shard_map.82 = bf16[16,192,128]{2,1,0:T(8,128)(2,1)S(1)} custom-call(s32[1]{0:T(128)S(6)} %copy.9.length_ref, bf16[8,128,128]{2,1,0:T(8,128)(2,1)S(1)} %copy-done.4, bf16[128,512]{1,0:T(8,128)(2,1)S(1)} %copy-done.5), custom_call_target="tpu_custom_call" | custom-call | flops 134217728 | bytes 1179652 | tf_op jit(solution)/shard_map/pallas_call | solution.py:190
  4.8 0.0 copy-start.8
  4.9 29.4 %all_to_all.15.came_ref = bf16[16,192,128]{2,1,0:T(8,128)(2,1)S(1)} all-to-all(bf16[16,192,128]{2,1,0:T(8,128)(2,1)S(1)} %shard_map.82), channel_id=1, replica_groups=mesh['dap'=16,'rep'=2] {'dap'}, dimensions={0} | all-to-all | bytes 1572864 | tf_op jit(solution)/shard_map/all_to_all | solution.py:206
  34.2 1.2 %shard_map.83 = bf16[16,64,128]{2,1,0:T(8,128)(2,1)} custom-call(bf16[16,192,128]{2,1,0:T(8,128)(2,1)S(1)} %all_to_all.15.came_ref), custom_call_target="tpu_custom_call" | custom-call | flops 33554432 | bytes 1048576 | tf_op jit(solution)/shard_map/pallas_call | solution.py:190
  35.4 0.0 copy-start.6
  35.4 3.7 %all-to-all-start.1 = ((bf16[16,64,128]{2,1,0:T(8,128)(2,1)}), bf16[16,64,128]{2,1,0:T(8,128)(2,1)S(1)}, u32[]{:S(2)}, u32[]{:S(2)}) async-start(bf16[16,64,128]{2,1,0:T(8,128)(2,1)} %shard_map.83), calls=%async_computation.1 | async-start | bytes 524288 | tf_op jit(solution)/shard_map/all_to_all | solution.py:206
  39.1 0.0 copy-done.12
  39.1 0.0 copy-done.7
  39.1 0.5 shard_map.84
  39.6 8.6 %all-to-all-done.1.came_ref = bf16[16,64,128]{2,1,0:T(8,128)(2,1)S(1)} async-done(((bf16[16,64,128]{2,1,0:T(8,128)(2,1)}), bf16[16,64,128]{2,1,0:T(8,128)(2,1)S(1)}, u32[]{:S(2)}, u32[]{:S(2)}) %all-to-all-start.1) | async-done | bytes 262176 | tf_op jit(solution)/shard_map/all_to_all | solution.py:206
  48.2 0.0 copy-done.8
  48.2 1.6 %shard_map.85 = (bf16[16,32,128]{2,1,0:T(8,128)(2,1)}, bf16[8,128,128]{2,1,0:T(8,128)(2,1)S(1)}, bf16[8,128,128]{2,1,0:T(8,128)(2,1)S(1)}) custom-call(bf16[16,64,128]{2,1,0:T(8,128)(2,1)S(1)} %all-to-all-done.1.came_ref, f32[8,128,128]{2,1,0:T(8,128)S(1)} %get-tuple-element.13.gate_ref, bf16[8,128,128]{2,1,0:T(8,128)(2,1)S(1)} %get-tuple-element.14.columns_ref, ...), custom_call_target="tpu_custom_call" | custom-call | flops 33554432 | bytes 1753088 | tf_op jit(solution)/shard_map/pallas_call | solution.py:190
  49.8 0.0 copy-start.2
  49.8 0.7 %copy-done.2 = bf16[8,128,128]{2,1,0:T(8,128)(2,1)} copy-done((bf16[8,128,128]{2,1,0:T(8,128)(2,1)}, bf16[8,128,128]{2,1,0:T(8,128)(2,1)S(1)}, u32[]{:S(2)}) %copy-start.2) | copy-done | bytes 262168
  50.5 0.0 copy-start.9
  50.5 0.7 %copy-done.9 = bf16[8,128,128]{2,1,0:T(8,128)(2,1)} copy-done((bf16[8,128,128]{2,1,0:T(8,128)(2,1)}, bf16[8,128,128]{2,1,0:T(8,128)(2,1)S(1)}, u32[]{:S(2)}) %copy-start.9) | copy-done | bytes 262168
  51.2 3.5 %all-to-all-start.2 = ((bf16[16,32,128]{2,1,0:T(8,128)(2,1)}), bf16[16,32,128]{2,1,0:T(8,128)(2,1)S(1)}, u32[]{:S(2)}, u32[]{:S(2)}) async-start(bf16[16,32,128]{2,1,0:T(8,128)(2,1)} %get-tuple-element.15), calls=%async_computation.2 | async-start | bytes 262144 | tf_op jit(solution)/shard_map/all_to_all | solution.py:206
  54.8 0.0 copy-start.10
  54.8 0.9 %copy-done.10 = bf16[8,128,128]{2,1,0:T(8,128)(2,1)S(1)} copy-done((bf16[8,128,128]{2,1,0:T(8,128)(2,1)S(1)}, bf16[8,128,128]{2,1,0:T(8,128)(2,1)}, u32[]{:S(2)}) %copy-start.10) | copy-done | bytes 262168
  55.7 0.0 copy-start.11
  55.7 0.9 %copy-done.11 = bf16[128,512]{1,0:T(8,128)(2,1)S(1)} copy-done((bf16[128,512]{1,0:T(8,128)(2,1)S(1)}, bf16[128,512]{1,0:T(8,128)(2,1)}, u32[]{:S(2)}) %copy-start.11) | copy-done | bytes 131096
  56.6 1.9 %shard_map.86 = (f32[8,512,128]{2,1,0:T(8,128)S(1)}, bf16[8,144,512]{2,1,0:T(8,128)(2,1)S(1)}, f32[8,128,128]{2,1,0:T(8,128)S(1)}) custom-call(s32[1]{0:T(128)S(6)} %copy.9.length_ref, bf16[8,128,128]{2,1,0:T(8,128)(2,1)S(1)} %copy-done.10, bf16[128,512]{1,0:T(8,128)(2,1)S(1)} %copy-done.11), custom_call_target="tpu_custom_call" | custom-call | flops 268435456 | bytes 4194308 | tf_op jit(solution)/shard_map/pallas_call | solution.py:190
  58.5 0.0 copy-start
  58.5 0.8 %copy-done = f32[8,128,128]{2,1,0:T(8,128)} copy-done((f32[8,128,128]{2,1,0:T(8,128)}, f32[8,128,128]{2,1,0:T(8,128)S(1)}, u32[]{:S(2)}) %copy-start) | copy-done | bytes 524312
  59.3 3.2 %all-to-all-done.2.bias_ref = bf16[16,32,128]{2,1,0:T(8,128)(2,1)S(1)} async-done(((bf16[16,32,128]{2,1,0:T(8,128)(2,1)}), bf16[16,32,128]{2,1,0:T(8,128)(2,1)S(1)}, u32[]{:S(2)}, u32[]{:S(2)}) %all-to-all-start.2) | async-done | bytes 131104 | tf_op jit(solution)/shard_map/all_to_all | solution.py:206
  62.6 0.0 copy-done.6
  62.6 0.0 copy-start.1
  62.6 1.0 %copy-done.1 = f32[8,128,128]{2,1,0:T(8,128)S(1)} copy-done((f32[8,128,128]{2,1,0:T(8,128)S(1)}, f32[8,128,128]{2,1,0:T(8,128)}, u32[]{:S(2)}) %copy-start.1) | copy-done | bytes 524312
  63.6 0.0 copy-start.3
  63.6 0.9 %copy-done.3 = bf16[8,128,128]{2,1,0:T(8,128)(2,1)S(1)} copy-done((bf16[8,128,128]{2,1,0:T(8,128)(2,1)S(1)}, bf16[8,128,128]{2,1,0:T(8,128)(2,1)}, u32[]{:S(2)}) %copy-start.3) | copy-done | bytes 262168
  64.6 1.8 %shard_map.87 = bf16[128,8,128]{2,1,0:T(8,128)(2,1)} custom-call(s32[1]{0:T(128)S(6)} %copy.9.length_ref, bf16[16,32,128]{2,1,0:T(8,128)(2,1)S(1)} %all-to-all-done.2.bias_ref, f32[8,512,128]{2,1,0:T(8,128)S(1)} %get-tuple-element.17.score_ref, bf16[8,144,512]{2,1,0:T(8,128)(2,1)S(1)} %get-tuple-element.18.v_ref, f32[8,128,128]{2,1,0:T(8,128)S(1)} %copy-done.1, ...), custom_call_target="tpu_custom_call" | custom-call | flops 268435456 | bytes 4489220 | tf_op jit(solution)/shard_map/pallas_call | solution.py:190
  (2 shorter events, 0.0 us)
Async XLA Ops:
  0.7 1.0 %copy-start.4 = (bf16[8,128,128]{2,1,0:T(8,128)(2,1)S(1)}, bf16[8,128,128]{2,1,0:T(8,128)(2,1)}, u32[]{:S(2)}) copy-start(bf16[8,128,128]{2,1,0:T(8,128)(2,1)} %pair_hbm.1) | copy-start | bytes 786436
  1.6 0.9 %copy-start.5 = (bf16[128,512]{1,0:T(8,128)(2,1)S(1)}, bf16[128,512]{1,0:T(8,128)(2,1)}, u32[]{:S(2)}) copy-start(bf16[128,512]{1,0:T(8,128)(2,1)} %w_hbm.1) | copy-start | bytes 393220
  2.5 36.6 %copy-start.12 = (bf16[128,4]{0,1:T(4,128)(2,1)S(1)}, bf16[128,4]{0,1:T(4,128)(2,1)}, u32[]{:S(2)}) copy-start(bf16[128,4]{0,1:T(4,128)(2,1)} %param.13) | copy-start | bytes 3076
  2.5 36.6 %copy-start.7 = (bf16[128,128]{1,0:T(8,128)(2,1)S(1)}, bf16[128,128]{1,0:T(8,128)(2,1)}, u32[]{:S(2)}) copy-start(bf16[128,128]{1,0:T(8,128)(2,1)} %w_ref.3) | copy-start | bytes 98308
  4.8 43.4 %copy-start.8 = (bf16[128,128]{1,0:T(8,128)(2,1)S(1)}, bf16[128,128]{1,0:T(8,128)(2,1)}, u32[]{:S(2)}) copy-start(bf16[128,128]{1,0:T(8,128)(2,1)} %w_out_ref.1) | copy-start | bytes 98308
  35.4 27.2 %copy-start.6 = (bf16[128,128]{1,0:T(8,128)(2,1)S(1)}, bf16[128,128]{1,0:T(8,128)(2,1)}, u32[]{:S(2)}) copy-start(bf16[128,128]{1,0:T(8,128)(2,1)} %w_ref.5) | copy-start | bytes 98308
  35.4 12.8 %all-to-all-start.1 = ((bf16[16,64,128]{2,1,0:T(8,128)(2,1)}), bf16[16,64,128]{2,1,0:T(8,128)(2,1)S(1)}, u32[]{:S(2)}, u32[]{:S(2)}) async-start(bf16[16,64,128]{2,1,0:T(8,128)(2,1)} %shard_map.83), calls=%async_computation.1 | async-start | bytes 524288 | tf_op jit(solution)/shard_map/all_to_all | solution.py:206
  49.8 0.7 %copy-start.2 = (bf16[8,128,128]{2,1,0:T(8,128)(2,1)}, bf16[8,128,128]{2,1,0:T(8,128)(2,1)S(1)}, u32[]{:S(2)}) copy-start(bf16[8,128,128]{2,1,0:T(8,128)(2,1)S(1)} %get-tuple-element.20.mid_ref) | copy-start | bytes 786436
  50.5 0.7 %copy-start.9 = (bf16[8,128,128]{2,1,0:T(8,128)(2,1)}, bf16[8,128,128]{2,1,0:T(8,128)(2,1)S(1)}, u32[]{:S(2)}) copy-start(bf16[8,128,128]{2,1,0:T(8,128)(2,1)S(1)} %get-tuple-element.16.normed_ref) | copy-start | bytes 786436
  51.2 11.3 %all-to-all-start.2 = ((bf16[16,32,128]{2,1,0:T(8,128)(2,1)}), bf16[16,32,128]{2,1,0:T(8,128)(2,1)S(1)}, u32[]{:S(2)}, u32[]{:S(2)}) async-start(bf16[16,32,128]{2,1,0:T(8,128)(2,1)} %get-tuple-element.15), calls=%async_computation.2 | async-start | bytes 262144 | tf_op jit(solution)/shard_map/all_to_all | solution.py:206
  54.8 1.0 %copy-start.10 = (bf16[8,128,128]{2,1,0:T(8,128)(2,1)S(1)}, bf16[8,128,128]{2,1,0:T(8,128)(2,1)}, u32[]{:S(2)}) copy-start(bf16[8,128,128]{2,1,0:T(8,128)(2,1)} %copy-done.9) | copy-start | bytes 786436
  55.7 0.9 %copy-start.11 = (bf16[128,512]{1,0:T(8,128)(2,1)S(1)}, bf16[128,512]{1,0:T(8,128)(2,1)}, u32[]{:S(2)}) copy-start(bf16[128,512]{1,0:T(8,128)(2,1)} %w_ref.4) | copy-start | bytes 393220
  58.5 0.8 %copy-start = (f32[8,128,128]{2,1,0:T(8,128)}, f32[8,128,128]{2,1,0:T(8,128)S(1)}, u32[]{:S(2)}) copy-start(f32[8,128,128]{2,1,0:T(8,128)S(1)} %get-tuple-element.19.gate_ref) | copy-start | bytes 1572868
  62.6 1.0 %copy-start.1 = (f32[8,128,128]{2,1,0:T(8,128)S(1)}, f32[8,128,128]{2,1,0:T(8,128)}, u32[]{:S(2)}) copy-start(f32[8,128,128]{2,1,0:T(8,128)} %copy-done) | copy-start | bytes 1572868
  63.6 0.9 %copy-start.3 = (bf16[8,128,128]{2,1,0:T(8,128)(2,1)S(1)}, bf16[8,128,128]{2,1,0:T(8,128)(2,1)}, u32[]{:S(2)}) copy-start(bf16[8,128,128]{2,1,0:T(8,128)(2,1)} %copy-done.2) | copy-start | bytes 786436

commit v4 on v3

--- a/solution.py
+++ b/solution.py
@@ -47,11 +47,10 @@
     first_row = lax.axis_index("dap") * rows
     length = length_ref[0]
     key_valid = jnp.where(lax.broadcasted_iota(jnp.int32, (1, count), 1) < length, 1.0, 0.0)
-    copies[0].wait()
+    for copy in copies:
+        copy.wait()
     w_turned = w_ref[...].T
     for r in range(rows):
-        if r % 2 == 0:
-            copies[1 + r // 2].wait()
         x = pair_ref[r].astype(F32)
         normed = layer_norm(x, 1).astype(BF16)
         projected = dot(w_turned, normed, 1, 1)
@@ -91,7 +90,7 @@
         gate_ref[j] = sigmoid(dot(layer_norm(x, 1).astype(BF16), w, 1, 0))
 
 
-def middle_kernel(came_ref, gate_ref, columns_ref, w_out_ref, w_bias_ref, bias_ref, normed_ref, mid_ref, wide_ref):
+def middle_kernel(came_ref, gate_ref, columns_ref, w_out_ref, w_bias_ref, bias_ref, mid_ref, wide_ref, normed_ref):
     columns, count, channels = mid_ref.shape
     blocks, per_block, _ = came_ref.shape
     hidden = blocks * per_block // columns
@@ -125,31 +124,28 @@
     bias_ref[...] = jnp.broadcast_to(total.astype(BF16)[None], bias_ref.shape)
 
 
-def heads_kernel(heads, length_ref, normed_ref, w_ref, score_ref, v_ref, gate_ref):
-    columns, count, channels = normed_ref.shape
+def heads_kernel(heads, length_ref, mid_ref, w_ref, score_ref, v_ref, gate_ref):
+    columns, count, channels = mid_ref.shape
     width = gate_ref.shape[1]
     size = width // heads
     w = w_ref[...]
     w_turned = w[:, 2 * width :].T
     lane = lax.broadcasted_iota(jnp.int32, (count, width), 1) // size
-    row = lax.broadcasted_iota(jnp.int32, (width, count), 0) // size
     valid = lax.broadcasted_iota(jnp.int32, (count, count), 0) < length_ref[0]
-    extra = (v_ref.shape[1] - width, heads * count)
-    extra_head = lax.broadcasted_iota(jnp.int32, extra, 1) // count
-    ones = jnp.where(lax.broadcasted_iota(jnp.int32, extra, 0) == extra_head, 1.0, 0.0).astype(BF16)
-    for j in range(columns):
-        normed = normed_ref[j]
+    ones = jnp.where(lax.broadcasted_iota(jnp.int32, (16, count), 0) == 0, 1.0, 0.0).astype(BF16)
+    for j in range(columns):
+        normed = layer_norm(mid_ref[j].astype(F32), 1).astype(BF16)
         qk = dot(normed, w[:, : 2 * width], 1, 0)
         q = qk[:, :width].astype(BF16)
         vg = dot(w_turned, normed, 1, 1)
         gate_ref[j] = sigmoid(vg[width:])
-        v_ref[j, width:, :] = ones
         for h in range(heads):
             own = slice(h * count, (h + 1) * count)
             k = jnp.where(lane == h, qk[:, width:], 0.0).astype(BF16)
             score = dot(k, q, 1, 1) * (size ** (-0.5) * LOG2E)
             score_ref[j, own, :] = jnp.where(valid, score, 0.0)
-            v_ref[j, :width, own] = jnp.where(row == h, vg[:width], 0.0).astype(BF16)
+            v_ref[j, h, :size, :] = vg[h * size : (h + 1) * size].astype(BF16)
+            v_ref[j, h, size:, :] = ones
 
 
 def attention_kernel(
@@ -172,11 +168,10 @@
         for j in range(columns):
             expo_ref[j, own, :] = jnp.exp2(score_ref[j, own, :] + bias - tops[j]).astype(BF16)
     for j in range(columns):
-        output = dot(v_ref[j], expo_ref[j], 1, 0)
-        scale = 1.0 / output[width : width + heads]
         for h in range(heads):
             own = slice(h * size, (h + 1) * size)
-            attended = gate_ref[j, own, :] * (output[own] * scale[h : h + 1])
+            output = dot(v_ref[j, h], expo_ref[j, h * count : (h + 1) * count, :], 1, 0)
+            attended = gate_ref[j, own, :] * (output[:size] * (1.0 / output[size : size + 1]))
             attended_ref[j, own, :] = attended.astype(BF16)
     w = w_ref[...]
     for j in range(columns):
@@ -217,7 +212,11 @@
     (sent,) = call(
         project_kernel,
         [shape((blocks, 24 * rows, count), BF16)],
-        (length, pair, w_proj),
+        (
+            length,
+            pltpu.with_memory_space_constraint(pair, pltpu.HBM),
+            pltpu.with_memory_space_constraint(w_proj, pltpu.HBM),
+        ),
         [SMEM, HBM, HBM],
         [
             pltpu.VMEM(pair.shape, BF16),
@@ -243,11 +242,11 @@
         flops=2 * pair.size * channels,
     )
     w_rows = jnp.repeat(w_bias.T, rows, axis=0).astype(F32)
-    bias, normed, mid = call(
+    bias, mid = call(
         middle_kernel,
-        [shape((blocks, heads * rows, count), BF16), shape(square, BF16), shape(square, BF16)],
+        [shape((blocks, heads * rows, count), BF16), shape(square, BF16)],
         (arrived, gate, columns, w_out, w_rows),
-        scratch=[wide],
+        scratch=[wide, pltpu.VMEM(square, BF16)],
         flops=2 * pair.size * channels,
     )
     bias = exchange(bias)
@@ -255,10 +254,10 @@
         functools.partial(heads_kernel, heads),
         [
             shape((rows, heads * count, count), F32),
-            shape((rows, width + 16, heads * count), BF16),
+            shape((rows, heads, width // heads + 16, count), BF16),
             shape((rows, width, count), F32),
         ],
-        (length, normed, w_qkvg),
+        (length, mid, w_qkvg),
         [SMEM, VMEM, VMEM],
         flops=2 * pair.size * 8 * width,
     )

time: 67 us -> 61.4 us (0.916)
  local copies, waits for them, and re-layouts: 7.9 us -> 0.92 us
  waiting for transfers between devices: 11.8 us -> 13.4 us
    unnamed x26 -> x10, local copies, waits for them, and re-layouts: 7.89 us -> 0.92 us
    all_to_all x2, waiting for transfers between devices: 11.8 us -> 13.4 us  [exchange(): return lax.all_to_all(x, 'dap', split_axis=0, concat_axis=0, tiled=True)]
where the time goes in v4:
time: 61.4 us; the launch traced here: 60.9 us
  blocking collectives  29.4 us (48%)
  waiting for transfers between devices  13.4 us (22%)
  Pallas kernels  9.22 us (15%)
  starting transfers between devices  7.2 us (12%)
  local copies, waits for them, and re-layouts  0.92 us (1%)
  between operations  0.76 us (1%)
    all_to_all x1, blocking collectives, exchange(): return lax.all_to_all(x, 'dap', split_axis=0, concat_axis=0, tiled=True)  29.4 us
    all_to_all x2, waiting for transfers between devices, exchange(): return lax.all_to_all(x, 'dap', split_axis=0, concat_axis=0, tiled=True)  13.4 us
    pallas_call x6, Pallas kernels, call(): pl.pallas_call(kernel, out_shape=[jax.ShapeDtypeStruct(o.shape, o.dtype)...  9.22 us
    all_to_all x2, starting transfers between devices, exchange(): return lax.all_to_all(x, 'dap', split_axis=0, concat_axis=0, tiled=True)  7.2 us
  transfers between devices with their start and end apart: 2, of which 2 were waited for; matrix products, arithmetic and copies ran while one was open for 0% of the time, Pallas kernels for 4%

profile of v4, /device:TPU:0, one launch (start us, length us, event | category | flops | bytes accessed | tf_op | source)
XLA Modules:
  0.0 60.9 jit_solution(4527522888019312591)
XLA Ops:
  0.7 0.0 copy-start.4
  0.7 0.0 copy-start.1
  0.7 2.0 %shard_map.82 = bf16[16,192,128]{2,1,0:T(8,128)(2,1)S(1)} custom-call(s32[1]{0:T(128)S(6)} %copy.9.length_ref, bf16[8,128,128]{2,1,0:T(8,128)(2,1)} %pair_hbm.1, bf16[128,512]{1,0:T(8,128)(2,1)} %w_hbm.1), custom_call_target="tpu_custom_call" | custom-call | flops 134217728 | bytes 1179652 | tf_op jit(solution)/shard_map/pallas_call | solution.py:185
  2.7 0.0 copy-start.2
  2.7 29.4 %all_to_all.15.came_ref = bf16[16,192,128]{2,1,0:T(8,128)(2,1)S(1)} all-to-all(bf16[16,192,128]{2,1,0:T(8,128)(2,1)S(1)} %shard_map.82), channel_id=1, replica_groups=mesh['dap'=16,'rep'=2] {'dap'}, dimensions={0} | all-to-all | bytes 1572864 | tf_op jit(solution)/shard_map/all_to_all | solution.py:201
  32.1 1.2 %shard_map.83 = bf16[16,64,128]{2,1,0:T(8,128)(2,1)} custom-call(bf16[16,192,128]{2,1,0:T(8,128)(2,1)S(1)} %all_to_all.15.came_ref), custom_call_target="tpu_custom_call" | custom-call | flops 33554432 | bytes 1048576 | tf_op jit(solution)/shard_map/pallas_call | solution.py:185
  33.2 0.0 copy-start
  33.2 3.7 %all-to-all-start.1 = ((bf16[16,64,128]{2,1,0:T(8,128)(2,1)}), bf16[16,64,128]{2,1,0:T(8,128)(2,1)S(1)}, u32[]{:S(2)}, u32[]{:S(2)}) async-start(bf16[16,64,128]{2,1,0:T(8,128)(2,1)} %shard_map.83), calls=%async_computation.1 | async-start | bytes 524288 | tf_op jit(solution)/shard_map/all_to_all | solution.py:201
  36.9 0.0 copy-done.4
  36.9 0.0 copy-done.1
  37.0 0.5 shard_map.84
  37.5 8.6 %all-to-all-done.1.came_ref = bf16[16,64,128]{2,1,0:T(8,128)(2,1)S(1)} async-done(((bf16[16,64,128]{2,1,0:T(8,128)(2,1)}), bf16[16,64,128]{2,1,0:T(8,128)(2,1)S(1)}, u32[]{:S(2)}, u32[]{:S(2)}) %all-to-all-start.1) | async-done | bytes 262176 | tf_op jit(solution)/shard_map/all_to_all | solution.py:201
  46.0 0.0 copy-done.2
  46.0 1.6 %shard_map.85 = (bf16[16,32,128]{2,1,0:T(8,128)(2,1)}, bf16[8,128,128]{2,1,0:T(8,128)(2,1)S(1)}) custom-call(bf16[16,64,128]{2,1,0:T(8,128)(2,1)S(1)} %all-to-all-done.1.came_ref, f32[8,128,128]{2,1,0:T(8,128)S(1)} %get-tuple-element.12.gate_ref, bf16[8,128,128]{2,1,0:T(8,128)(2,1)S(1)} %get-tuple-element.13.columns_ref, bf16[128,128]{1,0:T(8,128)(2,1)S(1)} %copy-done.2, ...), custom_call_target="tpu_custom_call" | custom-call | flops 33554432 | bytes 1490944 | tf_op jit(solution)/shard_map/pallas_call | solution.py:185
  47.7 3.5 %all-to-all-start.2 = ((bf16[16,32,128]{2,1,0:T(8,128)(2,1)}), bf16[16,32,128]{2,1,0:T(8,128)(2,1)S(1)}, u32[]{:S(2)}, u32[]{:S(2)}) async-start(bf16[16,32,128]{2,1,0:T(8,128)(2,1)} %get-tuple-element.14), calls=%async_computation.2 | async-start | bytes 262144 | tf_op jit(solution)/shard_map/all_to_all | solution.py:201
  51.2 0.0 copy-start.3
  51.3 0.9 %copy-done.3 = bf16[128,512]{1,0:T(8,128)(2,1)S(1)} copy-done((bf16[128,512]{1,0:T(8,128)(2,1)S(1)}, bf16[128,512]{1,0:T(8,128)(2,1)}, u32[]{:S(2)}) %copy-start.3) | copy-done | bytes 131096
  52.1 2.1 %shard_map.86 = (f32[8,512,128]{2,1,0:T(8,128)S(1)}, bf16[8,4,48,128]{3,2,1,0:T(8,128)(2,1)S(1)}, f32[8,128,128]{2,1,0:T(8,128)S(1)}) custom-call(s32[1]{0:T(128)S(6)} %copy.9.length_ref, bf16[8,128,128]{2,1,0:T(8,128)(2,1)S(1)} %get-tuple-element.15.mid_ref, bf16[128,512]{1,0:T(8,128)(2,1)S(1)} %copy-done.3), custom_call_target="tpu_custom_call" | custom-call | flops 268435456 | bytes 3407876 | tf_op jit(solution)/shard_map/pallas_call | solution.py:185
  54.2 4.8 %all-to-all-done.2.bias_ref = bf16[16,32,128]{2,1,0:T(8,128)(2,1)S(1)} async-done(((bf16[16,32,128]{2,1,0:T(8,128)(2,1)}), bf16[16,32,128]{2,1,0:T(8,128)(2,1)S(1)}, u32[]{:S(2)}, u32[]{:S(2)}) %all-to-all-start.2) | async-done | bytes 131104 | tf_op jit(solution)/shard_map/all_to_all | solution.py:201
  59.0 0.0 copy-done
  59.0 1.8 %shard_map.87 = bf16[128,8,128]{2,1,0:T(8,128)(2,1)} custom-call(s32[1]{0:T(128)S(6)} %copy.9.length_ref, bf16[16,32,128]{2,1,0:T(8,128)(2,1)S(1)} %all-to-all-done.2.bias_ref, f32[8,512,128]{2,1,0:T(8,128)S(1)} %get-tuple-element.16.score_ref, bf16[8,4,48,128]{3,2,1,0:T(8,128)(2,1)S(1)} %get-tuple-element.17.v_ref, ...), custom_call_target="tpu_custom_call" | custom-call | flops 268435456 | bytes 3702788 | tf_op jit(solution)/shard_map/pallas_call | solution.py:185
  (2 shorter events, 0.0 us)
Async XLA Ops:
  0.7 36.3 %copy-start.4 = (bf16[128,4]{0,1:T(4,128)(2,1)S(1)}, bf16[128,4]{0,1:T(4,128)(2,1)}, u32[]{:S(2)}) copy-start(bf16[128,4]{0,1:T(4,128)(2,1)} %param.13) | copy-start | bytes 3076
  0.7 36.3 %copy-start.1 = (bf16[128,128]{1,0:T(8,128)(2,1)S(1)}, bf16[128,128]{1,0:T(8,128)(2,1)}, u32[]{:S(2)}) copy-start(bf16[128,128]{1,0:T(8,128)(2,1)} %w_ref.3) | copy-start | bytes 98308
  2.7 43.4 %copy-start.2 = (bf16[128,128]{1,0:T(8,128)(2,1)S(1)}, bf16[128,128]{1,0:T(8,128)(2,1)}, u32[]{:S(2)}) copy-start(bf16[128,128]{1,0:T(8,128)(2,1)} %w_out_ref.1) | copy-start | bytes 98308
  33.2 25.8 %copy-start = (bf16[128,128]{1,0:T(8,128)(2,1)S(1)}, bf16[128,128]{1,0:T(8,128)(2,1)}, u32[]{:S(2)}) copy-start(bf16[128,128]{1,0:T(8,128)(2,1)} %w_ref.5) | copy-start | bytes 98308
  33.2 12.8 %all-to-all-start.1 = ((bf16[16,64,128]{2,1,0:T(8,128)(2,1)}), bf16[16,64,128]{2,1,0:T(8,128)(2,1)S(1)}, u32[]{:S(2)}, u32[]{:S(2)}) async-start(bf16[16,64,128]{2,1,0:T(8,128)(2,1)} %shard_map.83), calls=%async_computation.1 | async-start | bytes 524288 | tf_op jit(solution)/shard_map/all_to_all | solution.py:201
  47.7 11.3 %all-to-all-start.2 = ((bf16[16,32,128]{2,1,0:T(8,128)(2,1)}), bf16[16,32,128]{2,1,0:T(8,128)(2,1)S(1)}, u32[]{:S(2)}, u32[]{:S(2)}) async-start(bf16[16,32,128]{2,1,0:T(8,128)(2,1)} %get-tuple-element.14), calls=%async_computation.2 | async-start | bytes 262144 | tf_op jit(solution)/shard_map/all_to_all | solution.py:201
  51.2 0.9 %copy-start.3 = (bf16[128,512]{1,0:T(8,128)(2,1)S(1)}, bf16[128,512]{1,0:T(8,128)(2,1)}, u32[]{:S(2)}) copy-start(bf16[128,512]{1,0:T(8,128)(2,1)} %w_ref.4) | copy-start | bytes 393220

commit v5 on v1

--- a/solution.py
+++ b/solution.py
@@ -1,7 +1,25 @@
+import functools
+
 import jax
 import jax.numpy as jnp
 from jax import lax
+from jax.experimental import pallas as pl
+from jax.experimental.pallas import tpu as pltpu
 from jax.sharding import PartitionSpec as P
+
+VMEM = pl.BlockSpec(memory_space=pltpu.VMEM)
+SMEM = pl.BlockSpec(memory_space=pltpu.SMEM)
+HBM = pl.BlockSpec(memory_space=pltpu.HBM)
+BF16, F32 = jnp.bfloat16, jnp.float32
+LOG2E = 1.4426950408889634
+
+
+def dot(a, b, over_a, over_b):
+    return lax.dot_general(a, b, (((over_a,), (over_b,)), ((), ())), preferred_element_type=F32)
+
+
+def sigmoid(x):
+    return 0.5 * jnp.tanh(0.5 * x) + 0.5
 
 
 def layer_norm(x, axis):
@@ -11,15 +29,261 @@
     return centered * lax.rsqrt(spread + 1e-05)
 
 
+def interleave(a, b, blocks):
+    split = (blocks, a.shape[0] // blocks, a.shape[1])
+    return jnp.concatenate([a.reshape(split), b.reshape(split)], axis=1).astype(BF16)
+
+
+def project_kernel(
+    length_ref,
+    pair_hbm,
+    w_hbm,
+    w_gate_hbm,
+    w_bias_hbm,
+    out_ref,
+    gate_ref,
+    w_rows_ref,
+    pair_ref,
+    w_ref,
+    w_gate_ref,
+    w_bias_ref,
+    normed_ref,
+    sems,
+):
+    rows, count, channels = pair_ref.shape
+    blocks = out_ref.shape[0]
+    hidden = w_ref.shape[1] // 4
+    copies = [
+        pltpu.make_async_copy(pair_hbm, pair_ref, sems.at[0]),
+        pltpu.make_async_copy(w_hbm, w_ref, sems.at[1]),
+        pltpu.make_async_copy(w_gate_hbm, w_gate_ref, sems.at[2]),
+        pltpu.make_async_copy(w_bias_hbm, w_bias_ref, sems.at[3]),
+    ]
+    for copy in copies:
+        copy.start()
+    first_row = lax.axis_index("dap") * rows
+    length = length_ref[0]
+    key_valid = jnp.where(lax.broadcasted_iota(jnp.int32, (1, count), 1) < length, 1.0, 0.0)
+    for copy in copies:
+        copy.wait()
+    for r in range(rows):
+        normed_ref[r] = layer_norm(pair_ref[r].astype(F32), 1).astype(BF16)
+    w_turned = w_ref[...].T
+    for r in range(rows):
+        projected = dot(w_turned, normed_ref[r], 1, 1)
+        mask = key_valid * jnp.where(first_row + r < length, 1.0, 0.0)
+        left = sigmoid(projected[hidden : 2 * hidden]) * projected[:hidden] * mask
+        right = sigmoid(projected[3 * hidden :]) * projected[2 * hidden : 3 * hidden] * mask
+        out_ref[:, 16 * r : 16 * r + 16, :] = interleave(left, right, blocks)
+    w_gate = w_gate_ref[...]
+    for r in range(rows):
+        gate_ref[r] = sigmoid(dot(normed_ref[r], w_gate, 1, 0))
+    w_bias = w_bias_ref[...].astype(F32)
+    for h in range(w_bias.shape[0]):
+        w_rows_ref[h * rows : (h + 1) * rows, :] = jnp.broadcast_to(w_bias[h : h + 1], (rows, channels))
+
+
+def product_kernel(came_ref, out_ref, wide_ref):
+    blocks, per_block, count = came_ref.shape
+    for p in range(blocks):
+        wide_ref[p * per_block : (p + 1) * per_block, :] = came_ref[p].astype(F32)
+
+    def product(c):
+        left = wide_ref[pl.ds(c, count, stride=16), :].astype(BF16)
+        right = wide_ref[pl.ds(8 + c, count, stride=16), :].astype(BF16)
+        return dot(left, right, 1, 1)
+
+    for c in range(0, 8, 2):
+        out_ref[:, 8 * c : 8 * c + 16, :] = interleave(product(c), product(c + 1), blocks)
+
+
+def middle_kernel(came_ref, gate_ref, pair_ref, w_out_ref, w_rows_ref, out_ref, wide_ref, mid_ref, normed_ref):
+    rows, count, channels = pair_ref.shape
+    blocks, per_block, _ = came_ref.shape
+    hidden = blocks * per_block // rows
+
+    def load(p):
+        return came_ref[p].astype(F32).reshape(per_block // rows, rows, count)
+
+    mean = jnp.zeros((rows, count), F32)
+    for p in range(blocks):
+        mean += jnp.sum(load(p), axis=0)
+    mean = mean * (1.0 / hidden)
+    spread = jnp.zeros((rows, count), F32)
+    for p in range(blocks):
+        spread += jnp.sum(jnp.square(load(p) - mean), axis=0)
+    scale = lax.rsqrt(spread * (1.0 / hidden) + 1e-05)
+    for p in range(blocks):
+        part = (load(p) - mean) * scale
+        wide_ref[p * per_block : (p + 1) * per_block, :] = part.reshape(per_block, count)
+    w_out = w_out_ref[...]
+    for r in range(rows):
+        product = wide_ref[pl.ds(r, hidden, stride=rows), :].astype(BF16)
+        update = dot(product, w_out, 0, 0)
+        mid = (pair_ref[r].astype(F32) + gate_ref[r] * update).astype(BF16)
+        mid_ref[r] = mid.astype(F32)
+    for r in range(0, rows, 2):
+        out_ref[:, 8 * r : 8 * r + 16, :] = interleave(mid_ref[r], mid_ref[r + 1], blocks)
+    for r in range(rows):
+        normed_ref[r] = layer_norm(mid_ref[r], 1).astype(BF16)
+    w_bias = w_rows_ref[...]
+    own = lax.broadcasted_iota(jnp.int32, w_bias.shape, 0) % rows
+    bias = jnp.zeros((w_bias.shape[0], count), F32)
+    for r in range(rows):
+        bias += dot(jnp.where(own == r, w_bias, 0.0).astype(BF16), normed_ref[r], 1, 1)
+    out_ref[:, 8 * rows :, :] = jnp.broadcast_to(bias.astype(BF16)[None], (blocks,) + bias.shape)
+
+
+def attention_kernel(
+    heads,
+    length_ref,
+    came_ref,
+    w_ref,
+    w_out_ref,
+    out_ref,
+    wide_ref,
+    added_ref,
+    normed_ref,
+    q_ref,
+    k_ref,
+    v_ref,
+    gate_ref,
+    score_ref,
+    expo_ref,
+    attended_ref,
+):
+    columns, width, count = gate_ref.shape
+    size = width // heads
+    blocks, block = came_ref.shape[0], columns * columns
+    for p in range(blocks):
+        wide_ref[p * block : (p + 1) * block, :] = came_ref[p, :block].astype(F32)
+    for j in range(columns):
+        normed_ref[j] = layer_norm(wide_ref[pl.ds(j, count, stride=columns), :], 1).astype(BF16)
+    w = w_ref[...]
+    for j in range(columns):
+        qk = dot(normed_ref[j], w[:, : 2 * width], 1, 0)
+        q_ref[j] = qk[:, :width].astype(BF16)
+        k_ref[j] = qk[:, width:].astype(BF16)
+    w_turned = w[:, 2 * width :].T
+    ones = jnp.where(lax.broadcasted_iota(jnp.int32, (16, count), 0) == 0, 1.0, 0.0).astype(BF16)
+    for j in range(columns):
+        vg = dot(w_turned, normed_ref[j], 1, 1)
+        gate_ref[j] = sigmoid(vg[width:])
+        for h in range(heads):
+            v_ref[j, h, :size, :] = vg[h * size : (h + 1) * size].astype(BF16)
+            v_ref[j, h, size:, :] = ones
+    lane = lax.broadcasted_iota(jnp.int32, (count, width), 1) // size
+    valid = lax.broadcasted_iota(jnp.int32, (count, count), 0) < length_ref[0]
+    for h in range(heads):
+        own = slice(h * count, (h + 1) * count)
+        start = block + h * columns
+        bias = came_ref[:, start : start + columns, :].astype(F32).reshape(count, count) * LOG2E
+        own_lanes = jnp.where(lane == h, 1.0, 0.0).astype(BF16)
+        for j in range(columns):
+            scaled = dot(k_ref[j] * own_lanes, q_ref[j], 1, 1) * (size ** (-0.5) * LOG2E) + bias
+            score_ref[j, own, :] = jnp.where(valid, scaled, -1000000000.0 * LOG2E)
+    for h in range(heads):
+        own = slice(h * count, (h + 1) * count)
+        tops = [jnp.max(score_ref[j, own, :].reshape(-1, 8, count), axis=0) for j in range(columns)]
+        tops = [jnp.max(top, axis=0, keepdims=True) for top in tops]
+        for j in range(columns):
+            expo_ref[j, own, :] = jnp.exp2(score_ref[j, own, :] - tops[j]).astype(BF16)
+    for j in range(columns):
+        for h in range(heads):
+            own = slice(h * size, (h + 1) * size)
+            output = dot(v_ref[j, h], expo_ref[j, h * count : (h + 1) * count, :], 1, 0)
+            attended = gate_ref[j, own, :] * (output[:size] * (1.0 / output[size : size + 1]))
+            attended_ref[j, own, :] = attended.astype(BF16)
+    w_out = w_out_ref[...]
+    for j in range(columns):
+        added_ref[pl.ds(j, count, stride=columns), :] = dot(attended_ref[j], w_out, 0, 0)
+    out_ref[...] = (wide_ref[...] + added_ref[...]).reshape(count, columns, w_out.shape[1]).astype(BF16)
+
+
+def call(kernel, outs, operands, specs=None, scratch=()):
+    size = sum(a.size * a.dtype.itemsize for a in list(operands) + list(outs))
+    return pl.pallas_call(
+        kernel,
+        out_shape=[jax.ShapeDtypeStruct(o.shape, o.dtype) for o in outs],
+        in_specs=[VMEM] * len(operands) if specs is None else specs,
+        out_specs=[VMEM] * len(outs),
+        scratch_shapes=list(scratch),
+        cost_estimate=pl.CostEstimate(flops=0, bytes_accessed=size, transcendentals=0),
+        compiler_params=pltpu.CompilerParams(vmem_limit_bytes=24 * 2**20),
+    )(*operands)
+
+
+def shape(dims, dtype):
+    return jax.ShapeDtypeStruct(dims, dtype)
+
+
 def exchange(x):
     return lax.all_to_all(x, "dap", split_axis=0, concat_axis=0, tiled=True)
 
 
+def kernel_body(pair, w_proj, w_gate_out, w_out, w_qkvg, w_bias, w_att_out, length):
+    rows, count, channels = pair.shape
+    hidden = w_out.shape[0]
+    blocks = count // rows
+    heads, width = w_bias.shape[1], w_att_out.shape[0]
+    square = (rows, count, channels)
+    wide = pltpu.VMEM((rows * count, channels), F32)
+
+    sent, gate, w_rows = call(
+        project_kernel,
+        [shape((blocks, 16 * rows, count), BF16), shape(square, F32), shape((heads * rows, channels), F32)],
+        [length] + [pltpu.with_memory_space_constraint(x, pltpu.HBM) for x in (pair, w_proj, w_gate_out, w_bias.T)],
+        [SMEM] + [HBM] * 4,
+        [
+            pltpu.VMEM(pair.shape, BF16),
+            pltpu.VMEM(w_proj.shape, BF16),
+            pltpu.VMEM(w_gate_out.shape, BF16),
+            pltpu.VMEM((heads, channels), BF16),
+            pltpu.VMEM(square, BF16),
+            pltpu.SemaphoreType.DMA((4,)),
+        ],
+    )
+    came = exchange(sent)
+    (product,) = call(
+        product_kernel,
+        [shape((blocks, 8 * rows, count), BF16)],
+        (came,),
+        scratch=[pltpu.VMEM((blocks * 16 * rows, count), F32)],
+    )
+    came = exchange(product)
+    (sent,) = call(
+        middle_kernel,
+        [shape((blocks, (8 + heads) * rows, count), BF16)],
+        (came, gate, pair, w_out, w_rows),
+        scratch=[wide, pltpu.VMEM(square, F32), pltpu.VMEM(square, BF16)],
+    )
+    came = exchange(sent)
+    (out,) = call(
+        functools.partial(attention_kernel, heads),
+        [shape((count, rows, channels), BF16)],
+        (length, came, w_qkvg, w_att_out),
+        [SMEM] + [VMEM] * 3,
+        [
+            wide,
+            wide,
+            pltpu.VMEM(square, BF16),
+            pltpu.VMEM((rows, count, width), BF16),
+            pltpu.VMEM((rows, count, width), BF16),
+            pltpu.VMEM((rows, heads, width // heads + 16, count), BF16),
+            pltpu.VMEM((rows, width, count), F32),
+            pltpu.VMEM((rows, heads * count, count), F32),
+            pltpu.VMEM((rows, heads * count, count), BF16),
+            pltpu.VMEM((rows, width, count), BF16),
+        ],
+    )
+    return out
+
+
 def matmul(spec, a, b):
     return jnp.einsum(spec, a, b, preferred_element_type=jnp.float32)
 
 
-def body(pair, w_proj, w_gate_out, w_out, w_qkvg, w_bias, w_att_out, length):
+def whole_body(pair, w_proj, w_gate_out, w_out, w_qkvg, w_bias, w_att_out, length):
     row_count, full_count, channels = pair.shape
     hidden = w_out.shape[0]
     device_count = full_count // row_count
@@ -92,6 +356,14 @@
     return result.astype(jnp.bfloat16)
 
 
+def body(pair, w_proj, w_gate_out, w_out, w_qkvg, w_bias, w_att_out, length):
+    rows, count, channels = pair.shape
+    share = w_out.shape[0] * rows // count
+    fits = share == rows == 8 and count == channels == w_att_out.shape[0] == 128
+    chosen = kernel_body if fits else whole_body
+    return chosen(pair, w_proj, w_gate_out, w_out, w_qkvg, w_bias, w_att_out, length)
+
+
 def solution(mesh):
     placed = (P(("rep", "dap"), None, None), P(), P(), P(), P(), P(), P(), P("rep"))
     return jax.shard_map(

time: 72.5 us -> 58.6 us (0.81)
  blocking collectives: 0 us -> 51.4 us
  waiting for transfers between devices: 30.5 us -> 0 us
  starting transfers between devices: 17.4 us -> 0 us
  matrix products: 8.58 us -> 0 us
  local copies, waits for them, and re-layouts: 8.24 us -> 0.03 us
  other arithmetic: 6.27 us -> 0 us
  Pallas kernels: 0 us -> 6.17 us
    all_to_all x0 -> x3, blocking collectives: none -> 51.4 us  [exchange(): return lax.all_to_all(x, 'dap', split_axis=0, concat_axis=0, tiled=True)]
    all_to_all x3 -> x0, waiting for transfers between devices: 30.5 us -> none  [exchange(): return lax.all_to_all(x, 'dap', split_axis=0, concat_axis=0, tiled=True)]
    all_to_all x3 -> x0, starting transfers between devices: 17.4 us -> none  [exchange(): return lax.all_to_all(x, 'dap', split_axis=0, concat_axis=0, tiled=True)]
    pallas_call x0 -> x4, Pallas kernels: none -> 6.17 us  [call(): pl.pallas_call(kernel, out_shape=[jax.ShapeDtypeStruct(o.shape, o.dtype)...]
    dot_general x8 -> x0, matrix products: 5.28 us -> none  [matmul(): return jnp.einsum(spec, a, b, preferred_element_type=jnp.float32)]
    reduce_sum x7 -> x0, other arithmetic: 3.36 us -> none  [the longest x4 1.89 us: layer_norm(): spread = jnp.mean(centered * centered, axis=axis, keepdims=True)]
    sub x1 -> x0, matrix products: 3.3 us -> none  [body(): expo = jnp.exp(score - top)]
    slice x5 -> x0, local copies, waits for them, and re-layouts: 2.84 us -> none  [the longest x2 1.05 us: body(): keys = mixed[..., width:2 * width].astype(jnp.bfloat16).reshape(per_head)]
  transfers between devices with their start and end apart: 3 -> 0, of which waited for: 3 -> 0; matrix products, arithmetic and copies ran while one was open for 8% -> 0% of each run, Pallas kernels for 0% -> 0%
where the time goes in v5:
time: 58.6 us; the launch traced here: 58.3 us
  blocking collectives  51.4 us (88%)
  Pallas kernels  6.17 us (11%)
  between operations  0.71 us (1%)
    all_to_all x3, blocking collectives, exchange(): return lax.all_to_all(x, 'dap', split_axis=0, concat_axis=0, tiled=True)  51.4 us
    pallas_call x4, Pallas kernels, call(): pl.pallas_call(kernel, out_shape=[jax.ShapeDtypeStruct(o.shape, o.dtype)...  6.17 us

profile of v5, /device:TPU:0, one launch (start us, length us, event | category | flops | bytes accessed | tf_op | source)
XLA Modules:
  0.0 58.3 jit_solution(9670755891758606479)
XLA Ops:
  0.7 2.1 %shard_map.82 = (bf16[16,128,128]{2,1,0:T(8,128)(2,1)S(1)}, f32[8,128,128]{2,1,0:T(8,128)S(1)}, f32[32,128]{1,0:T(8,128)S(1)}) custom-call(s32[1]{0:T(128)S(6)} %copy.9.length_ref, bf16[8,128,128]{2,1,0:T(8,128)(2,1)} %pair_ref.1, bf16[128,512]{1,0:T(8,128)(2,1)} %w_hbm.1, bf16[128,128]{1,0:T(8,128)(2,1)} %w_gate_hbm.1, bf16[4,128]{1,0:T(4,128)(2,1)} %bitcast.1), custom_call_target="tpu_custom_call" | custom-call | bytes 1491972 | tf_op jit(solution)/shard_map/pallas_call | solution.py:205
  2.8 23.3 %all_to_all.15.came_ref = bf16[16,128,128]{2,1,0:T(8,128)(2,1)S(1)} all-to-all(bf16[16,128,128]{2,1,0:T(8,128)(2,1)S(1)} %get-tuple-element.8), channel_id=1, replica_groups=mesh['dap'=16,'rep'=2] {'dap'}, dimensions={0} | all-to-all | bytes 1048576 | tf_op jit(solution)/shard_map/all_to_all | solution.py:221
  26.0 0.4 shard_map.83
  26.5 0.0 copy-start
  26.5 0.0 copy-start.2
  26.5 12.9 %all_to_all.16.came_ref = bf16[16,64,128]{2,1,0:T(8,128)(2,1)S(1)} all-to-all(bf16[16,64,128]{2,1,0:T(8,128)(2,1)S(1)} %shard_map.83), channel_id=1, replica_groups=mesh['dap'=16,'rep'=2] {'dap'}, dimensions={0} | all-to-all | bytes 524288 | tf_op jit(solution)/shard_map/all_to_all | solution.py:221
  39.4 0.0 copy-done
  39.4 0.0 copy-done.2
  39.4 1.0 %shard_map.84 = bf16[16,96,128]{2,1,0:T(8,128)(2,1)S(1)} custom-call(bf16[16,64,128]{2,1,0:T(8,128)(2,1)S(1)} %all_to_all.16.came_ref, f32[8,128,128]{2,1,0:T(8,128)S(1)} %get-tuple-element.9.gate_ref, bf16[8,128,128]{2,1,0:T(8,128)(2,1)S(1)} %copy-done, bf16[128,128]{1,0:T(8,128)(2,1)S(1)} %copy-done.2, f32[32,128]{1,0:T(8,128)S(1)} %get-tuple-element.10.w_rows_ref), custom_call_target="tpu_custom_call" | custom-call | bytes 1490944 | tf_op jit(solution)/shard_map/pallas_call | solution.py:205
  40.4 0.0 copy-start.1
  40.4 0.0 copy-start.3
  40.4 15.2 %all_to_all.17.came_ref = bf16[16,96,128]{2,1,0:T(8,128)(2,1)S(1)} all-to-all(bf16[16,96,128]{2,1,0:T(8,128)(2,1)S(1)} %shard_map.84), channel_id=1, replica_groups=mesh['dap'=16,'rep'=2] {'dap'}, dimensions={0} | all-to-all | bytes 786432 | tf_op jit(solution)/shard_map/all_to_all | solution.py:221
  55.6 0.0 copy-done.1
  55.6 0.0 copy-done.3
  55.6 2.6 %shard_map.85 = bf16[128,8,128]{2,1,0:T(8,128)(2,1)} custom-call(s32[1]{0:T(128)S(6)} %copy.9.length_ref, bf16[16,96,128]{2,1,0:T(8,128)(2,1)S(1)} %all_to_all.17.came_ref, bf16[128,512]{1,0:T(8,128)(2,1)S(1)} %copy-done.1, bf16[128,128]{1,0:T(8,128)(2,1)S(1)} %copy-done.3), custom_call_target="tpu_custom_call" | custom-call | bytes 819204 | tf_op jit(solution)/shard_map/pallas_call | solution.py:205
Async XLA Ops:
  26.5 13.0 %copy-start = (bf16[8,128,128]{2,1,0:T(8,128)(2,1)S(1)}, bf16[8,128,128]{2,1,0:T(8,128)(2,1)}, u32[]{:S(2)}) copy-start(bf16[8,128,128]{2,1,0:T(8,128)(2,1)} %pair_ref.1) | copy-start | bytes 786436
  26.5 12.9 %copy-start.2 = (bf16[128,128]{1,0:T(8,128)(2,1)S(1)}, bf16[128,128]{1,0:T(8,128)(2,1)}, u32[]{:S(2)}) copy-start(bf16[128,128]{1,0:T(8,128)(2,1)} %w_out_ref.2) | copy-start | bytes 98308
  40.4 15.2 %copy-start.1 = (bf16[128,512]{1,0:T(8,128)(2,1)S(1)}, bf16[128,512]{1,0:T(8,128)(2,1)}, u32[]{:S(2)}) copy-start(bf16[128,512]{1,0:T(8,128)(2,1)} %w_ref.1) | copy-start | bytes 393220
  40.4 15.2 %copy-start.3 = (bf16[128,128]{1,0:T(8,128)(2,1)S(1)}, bf16[128,128]{1,0:T(8,128)(2,1)}, u32[]{:S(2)}) copy-start(bf16[128,128]{1,0:T(8,128)(2,1)} %w_out_ref.3) | copy-start | bytes 98308

commit v6 on v5

--- a/solution.py
+++ b/solution.py
@@ -12,6 +12,7 @@
 HBM = pl.BlockSpec(memory_space=pltpu.HBM)
 BF16, F32 = jnp.bfloat16, jnp.float32
 LOG2E = 1.4426950408889634
+ORDER = [4, 0, 12, 8, 14, 10, 6, 2, 5, 1, 13, 9, 15, 11, 7, 3]
 
 
 def dot(a, b, over_a, over_b):
@@ -27,6 +28,11 @@
     centered = x - mean
     spread = jnp.mean(centered * centered, axis=axis, keepdims=True)
     return centered * lax.rsqrt(spread + 1e-05)
+
+
+def by_block(x, order):
+    size = x.shape[0] // len(order)
+    return jnp.concatenate([x[d * size : (d + 1) * size] for d in order], axis=0)
 
 
 def interleave(a, b, blocks):
@@ -97,7 +103,7 @@
         out_ref[:, 8 * c : 8 * c + 16, :] = interleave(product(c), product(c + 1), blocks)
 
 
-def middle_kernel(came_ref, gate_ref, pair_ref, w_out_ref, w_rows_ref, out_ref, wide_ref, mid_ref, normed_ref):
+def middle_kernel(order, came_ref, gate_ref, pair_ref, w_out_ref, w_rows_ref, out_ref, wide_ref, mid_ref, normed_ref):
     rows, count, channels = pair_ref.shape
     blocks, per_block, _ = came_ref.shape
     hidden = blocks * per_block // rows
@@ -120,7 +126,8 @@
     for r in range(rows):
         product = wide_ref[pl.ds(r, hidden, stride=rows), :].astype(BF16)
         update = dot(product, w_out, 0, 0)
-        mid = (pair_ref[r].astype(F32) + gate_ref[r] * update).astype(BF16)
+        pair, gate = by_block(pair_ref[r].astype(F32), order), by_block(gate_ref[r], order)
+        mid = (pair + gate * update).astype(BF16)
         mid_ref[r] = mid.astype(F32)
     for r in range(0, rows, 2):
         out_ref[:, 8 * r : 8 * r + 16, :] = interleave(mid_ref[r], mid_ref[r + 1], blocks)
@@ -135,6 +142,7 @@
 
 
 def attention_kernel(
+    order,
     heads,
     length_ref,
     came_ref,
@@ -173,7 +181,8 @@
             v_ref[j, h, :size, :] = vg[h * size : (h + 1) * size].astype(BF16)
             v_ref[j, h, size:, :] = ones
     lane = lax.broadcasted_iota(jnp.int32, (count, width), 1) // size
-    valid = lax.broadcasted_iota(jnp.int32, (count, count), 0) < length_ref[0]
+    token = by_block(lax.broadcasted_iota(jnp.int32, (count, count), 0), order)
+    valid = token < length_ref[0]
     for h in range(heads):
         own = slice(h * count, (h + 1) * count)
         start = block + h * columns
@@ -197,7 +206,10 @@
     w_out = w_out_ref[...]
     for j in range(columns):
         added_ref[pl.ds(j, count, stride=columns), :] = dot(attended_ref[j], w_out, 0, 0)
-    out_ref[...] = (wide_ref[...] + added_ref[...]).reshape(count, columns, w_out.shape[1]).astype(BF16)
+    for p, d in enumerate(order):
+        rows = slice(p * block, (p + 1) * block)
+        result = (wide_ref[rows, :] + added_ref[rows, :]).reshape(-1, columns, w_out.shape[1])
+        out_ref[d * columns : (d + 1) * columns] = result.astype(BF16)
 
 
 def call(kernel, outs, operands, specs=None, scratch=()):
@@ -217,8 +229,9 @@
     return jax.ShapeDtypeStruct(dims, dtype)
 
 
-def exchange(x):
-    return lax.all_to_all(x, "dap", split_axis=0, concat_axis=0, tiled=True)
+def exchange(x, order=None):
+    groups = None if order is None else [order]
+    return lax.all_to_all(x, "dap", split_axis=0, concat_axis=0, tiled=True, axis_index_groups=groups)
 
 
 def kernel_body(pair, w_proj, w_gate_out, w_out, w_qkvg, w_bias, w_att_out, length):
@@ -243,23 +256,23 @@
             pltpu.SemaphoreType.DMA((4,)),
         ],
     )
-    came = exchange(sent)
+    came = exchange(sent, ORDER)
     (product,) = call(
         product_kernel,
         [shape((blocks, 8 * rows, count), BF16)],
         (came,),
         scratch=[pltpu.VMEM((blocks * 16 * rows, count), F32)],
     )
-    came = exchange(product)
+    came = exchange(product, ORDER)
     (sent,) = call(
-        middle_kernel,
+        functools.partial(middle_kernel, ORDER),
         [shape((blocks, (8 + heads) * rows, count), BF16)],
         (came, gate, pair, w_out, w_rows),
         scratch=[wide, pltpu.VMEM(square, F32), pltpu.VMEM(square, BF16)],
     )
-    came = exchange(sent)
+    came = exchange(sent, ORDER)
     (out,) = call(
-        functools.partial(attention_kernel, heads),
+        functools.partial(attention_kernel, ORDER, heads),
         [shape((count, rows, channels), BF16)],
         (length, came, w_qkvg, w_att_out),
         [SMEM] + [VMEM] * 3,
@@ -359,7 +372,7 @@
 def body(pair, w_proj, w_gate_out, w_out, w_qkvg, w_bias, w_att_out, length):
     rows, count, channels = pair.shape
     share = w_out.shape[0] * rows // count
-    fits = share == rows == 8 and count == channels == w_att_out.shape[0] == 128
+    fits = share == rows == 8 and count // rows == len(ORDER) and count == channels == w_att_out.shape[0] == 128
     chosen = kernel_body if fits else whole_body
     return chosen(pair, w_proj, w_gate_out, w_out, w_qkvg, w_bias, w_att_out, length)
 

time: 58.6 us -> 53 us (0.904)
  blocking collectives: 51.4 us -> 45.9 us
    all_to_all x3, blocking collectives: 51.4 us -> 45.9 us  [exchange(): lax.all_to_all(x, 'dap', split_axis=0, concat_axis=0, tiled=True, axis_in...]
where the time goes in v6:
time: 53 us; the launch traced here: 52.8 us
  blocking collectives  45.9 us (87%)
  Pallas kernels  6.17 us (12%)
  between operations  0.71 us (1%)
    all_to_all x3, blocking collectives, exchange(): lax.all_to_all(x, 'dap', split_axis=0, concat_axis=0, tiled=True, axis_in...  45.9 us
    pallas_call x4, Pallas kernels, call(): pl.pallas_call(kernel, out_shape=[jax.ShapeDtypeStruct(o.shape, o.dtype)...  6.17 us

profile of v6, /device:TPU:0, one launch (start us, length us, event | category | flops | bytes accessed | tf_op | source)
XLA Modules:
  0.0 52.8 jit_solution(644922411939169223)
XLA Ops:
  0.7 2.1 %shard_map.82 = (bf16[16,128,128]{2,1,0:T(8,128)(2,1)S(1)}, f32[8,128,128]{2,1,0:T(8,128)S(1)}, f32[32,128]{1,0:T(8,128)S(1)}) custom-call(s32[1]{0:T(128)S(6)} %copy.9.length_ref, bf16[8,128,128]{2,1,0:T(8,128)(2,1)} %pair_ref.1, bf16[128,512]{1,0:T(8,128)(2,1)} %w_hbm.1, bf16[128,128]{1,0:T(8,128)(2,1)} %w_gate_hbm.1, bf16[4,128]{1,0:T(4,128)(2,1)} %bitcast.1), custom_call_target="tpu_custom_call" | custom-call | bytes 1491972 | tf_op jit(solution)/shard_map/pallas_call | solution.py:217
  2.8 20.1 %all_to_all.15.came_ref = bf16[16,128,128]{2,1,0:T(8,128)(2,1)S(1)} all-to-all(bf16[16,128,128]{2,1,0:T(8,128)(2,1)S(1)} %get-tuple-element.8), channel_id=1, replica_groups={{8,0,24,16,28,20,12,4,10,2,26,18,30,22,14,6},{9,1,25,17,29,21,13,5,11,3..., dimensions={0} | all-to-all | bytes 1048576 | tf_op jit(solution)/shard_map/all_to_all | solution.py:234
  22.8 0.4 shard_map.83
  23.3 0.0 copy-start
  23.3 0.0 copy-start.2
  23.3 13.5 %all_to_all.16.came_ref = bf16[16,64,128]{2,1,0:T(8,128)(2,1)S(1)} all-to-all(bf16[16,64,128]{2,1,0:T(8,128)(2,1)S(1)} %shard_map.83), channel_id=1, replica_groups={{8,0,24,16,28,20,12,4,10,2,26,18,30,22,14,6},{9,1,25,17,29,21,13,5,11,3..., dimensions={0} | all-to-all | bytes 524288 | tf_op jit(solution)/shard_map/all_to_all | solution.py:234
  36.8 0.0 copy-done
  36.8 0.0 copy-done.2
  36.8 1.0 %shard_map.84 = bf16[16,96,128]{2,1,0:T(8,128)(2,1)S(1)} custom-call(bf16[16,64,128]{2,1,0:T(8,128)(2,1)S(1)} %all_to_all.16.came_ref, f32[8,128,128]{2,1,0:T(8,128)S(1)} %get-tuple-element.9.gate_ref, bf16[8,128,128]{2,1,0:T(8,128)(2,1)S(1)} %copy-done, bf16[128,128]{1,0:T(8,128)(2,1)S(1)} %copy-done.2, f32[32,128]{1,0:T(8,128)S(1)} %get-tuple-element.10.w_rows_ref), custom_call_target="tpu_custom_call" | custom-call | bytes 1490944 | tf_op jit(solution)/shard_map/pallas_call | solution.py:217
  37.8 0.0 copy-start.1
  37.9 0.0 copy-start.3
  37.9 12.2 %all_to_all.17.came_ref = bf16[16,96,128]{2,1,0:T(8,128)(2,1)S(1)} all-to-all(bf16[16,96,128]{2,1,0:T(8,128)(2,1)S(1)} %shard_map.84), channel_id=1, replica_groups={{8,0,24,16,28,20,12,4,10,2,26,18,30,22,14,6},{9,1,25,17,29,21,13,5,11,3..., dimensions={0} | all-to-all | bytes 786432 | tf_op jit(solution)/shard_map/all_to_all | solution.py:234
  50.1 0.0 copy-done.1
  50.1 0.0 copy-done.3
  50.1 2.6 %shard_map.85 = bf16[128,8,128]{2,1,0:T(8,128)(2,1)} custom-call(s32[1]{0:T(128)S(6)} %copy.9.length_ref, bf16[16,96,128]{2,1,0:T(8,128)(2,1)S(1)} %all_to_all.17.came_ref, bf16[128,512]{1,0:T(8,128)(2,1)S(1)} %copy-done.1, bf16[128,128]{1,0:T(8,128)(2,1)S(1)} %copy-done.3), custom_call_target="tpu_custom_call" | custom-call | bytes 819204 | tf_op jit(solution)/shard_map/pallas_call | solution.py:217
Async XLA Ops:
  23.3 13.6 %copy-start = (bf16[8,128,128]{2,1,0:T(8,128)(2,1)S(1)}, bf16[8,128,128]{2,1,0:T(8,128)(2,1)}, u32[]{:S(2)}) copy-start(bf16[8,128,128]{2,1,0:T(8,128)(2,1)} %pair_ref.1) | copy-start | bytes 786436
  23.3 13.5 %copy-start.2 = (bf16[128,128]{1,0:T(8,128)(2,1)S(1)}, bf16[128,128]{1,0:T(8,128)(2,1)}, u32[]{:S(2)}) copy-start(bf16[128,128]{1,0:T(8,128)(2,1)} %w_out_ref.2) | copy-start | bytes 98308
  37.8 12.3 %copy-start.1 = (bf16[128,512]{1,0:T(8,128)(2,1)S(1)}, bf16[128,512]{1,0:T(8,128)(2,1)}, u32[]{:S(2)}) copy-start(bf16[128,512]{1,0:T(8,128)(2,1)} %w_ref.1) | copy-start | bytes 393220
  37.9 12.3 %copy-start.3 = (bf16[128,128]{1,0:T(8,128)(2,1)S(1)}, bf16[128,128]{1,0:T(8,128)(2,1)}, u32[]{:S(2)}) copy-start(bf16[128,128]{1,0:T(8,128)(2,1)} %w_out_ref.3) | copy-start | bytes 98308

commit v7 on v5

--- a/solution.py
+++ b/solution.py
@@ -12,6 +12,10 @@
 HBM = pl.BlockSpec(memory_space=pltpu.HBM)
 BF16, F32 = jnp.bfloat16, jnp.float32
 LOG2E = 1.4426950408889634
+ORDERS = [
+    [4, 0, 12, 8, 14, 10, 6, 2, 5, 1, 13, 9, 15, 11, 7, 3],
+    [6, 10, 5, 2, 1, 11, 15, 3, 4, 8, 12, 0, 14, 7, 13, 9],
+]
 
 
 def dot(a, b, over_a, over_b):
@@ -27,6 +31,11 @@
     centered = x - mean
     spread = jnp.mean(centered * centered, axis=axis, keepdims=True)
     return centered * lax.rsqrt(spread + 1e-05)
+
+
+def devices(orders):
+    first = lax.axis_index("rep") == 0
+    return [jnp.where(first, jnp.int32(a), jnp.int32(b)) for a, b in zip(*orders)]
 
 
 def interleave(a, b, blocks):
@@ -97,8 +106,9 @@
         out_ref[:, 8 * c : 8 * c + 16, :] = interleave(product(c), product(c + 1), blocks)
 
 
-def middle_kernel(came_ref, gate_ref, pair_ref, w_out_ref, w_rows_ref, out_ref, wide_ref, mid_ref, normed_ref):
+def middle_kernel(orders, came_ref, gate_ref, pair_ref, w_out_ref, w_rows_ref, out_ref, wide_ref, mid_ref, normed_ref):
     rows, count, channels = pair_ref.shape
+    starts = [pl.multiple_of(d * rows, rows) for d in devices(orders)]
     blocks, per_block, _ = came_ref.shape
     hidden = blocks * per_block // rows
 
@@ -118,10 +128,16 @@
         wide_ref[p * per_block : (p + 1) * per_block, :] = part.reshape(per_block, count)
     w_out = w_out_ref[...]
     for r in range(rows):
+        mid_ref[r] = pair_ref[r].astype(F32)
+
+    def by_block(r):
+        return jnp.concatenate([mid_ref[r, pl.ds(start, rows), :] for start in starts], axis=0)
+
+    for r in range(rows):
         product = wide_ref[pl.ds(r, hidden, stride=rows), :].astype(BF16)
         update = dot(product, w_out, 0, 0)
-        mid = (pair_ref[r].astype(F32) + gate_ref[r] * update).astype(BF16)
-        mid_ref[r] = mid.astype(F32)
+        gate = jnp.concatenate([gate_ref[r, pl.ds(start, rows), :] for start in starts], axis=0)
+        mid_ref[r] = (by_block(r) + gate * update).astype(BF16).astype(F32)
     for r in range(0, rows, 2):
         out_ref[:, 8 * r : 8 * r + 16, :] = interleave(mid_ref[r], mid_ref[r + 1], blocks)
     for r in range(rows):
@@ -135,6 +151,7 @@
 
 
 def attention_kernel(
+    orders,
     heads,
     length_ref,
     came_ref,
@@ -173,7 +190,10 @@
             v_ref[j, h, :size, :] = vg[h * size : (h + 1) * size].astype(BF16)
             v_ref[j, h, size:, :] = ones
     lane = lax.broadcasted_iota(jnp.int32, (count, width), 1) // size
-    valid = lax.broadcasted_iota(jnp.int32, (count, count), 0) < length_ref[0]
+    own_devices = devices(orders)
+    within = lax.broadcasted_iota(jnp.int32, (columns, count), 0)
+    token = jnp.concatenate([within + d * columns for d in own_devices], axis=0)
+    valid = token < length_ref[0]
     for h in range(heads):
         own = slice(h * count, (h + 1) * count)
         start = block + h * columns
@@ -197,7 +217,10 @@
     w_out = w_out_ref[...]
     for j in range(columns):
         added_ref[pl.ds(j, count, stride=columns), :] = dot(attended_ref[j], w_out, 0, 0)
-    out_ref[...] = (wide_ref[...] + added_ref[...]).reshape(count, columns, w_out.shape[1]).astype(BF16)
+    for p, d in enumerate(own_devices):
+        rows = slice(p * block, (p + 1) * block)
+        result = (wide_ref[rows, :] + added_ref[rows, :]).reshape(-1, columns, w_out.shape[1])
+        out_ref[pl.ds(pl.multiple_of(d * columns, columns), columns)] = result.astype(BF16)
 
 
 def call(kernel, outs, operands, specs=None, scratch=()):
@@ -217,8 +240,11 @@
     return jax.ShapeDtypeStruct(dims, dtype)
 
 
-def exchange(x):
-    return lax.all_to_all(x, "dap", split_axis=0, concat_axis=0, tiled=True)
+def exchange(x, orders=None):
+    if orders is None:
+        return lax.all_to_all(x, "dap", split_axis=0, concat_axis=0, tiled=True)
+    groups = [[rep * len(order) + d for d in order] for rep, order in enumerate(orders)]
+    return lax.all_to_all(x, ("rep", "dap"), split_axis=0, concat_axis=0, tiled=True, axis_index_groups=groups)
 
 
 def kernel_body(pair, w_proj, w_gate_out, w_out, w_qkvg, w_bias, w_att_out, length):
@@ -243,23 +269,23 @@
             pltpu.SemaphoreType.DMA((4,)),
         ],
     )
-    came = exchange(sent)
+    came = exchange(sent, ORDERS)
     (product,) = call(
         product_kernel,
         [shape((blocks, 8 * rows, count), BF16)],
         (came,),
         scratch=[pltpu.VMEM((blocks * 16 * rows, count), F32)],
     )
-    came = exchange(product)
+    came = exchange(product, ORDERS)
     (sent,) = call(
-        middle_kernel,
+        functools.partial(middle_kernel, ORDERS),
         [shape((blocks, (8 + heads) * rows, count), BF16)],
         (came, gate, pair, w_out, w_rows),
         scratch=[wide, pltpu.VMEM(square, F32), pltpu.VMEM(square, BF16)],
     )
-    came = exchange(sent)
+    came = exchange(sent, ORDERS)
     (out,) = call(
-        functools.partial(attention_kernel, heads),
+        functools.partial(attention_kernel, ORDERS, heads),
         [shape((count, rows, channels), BF16)],
         (length, came, w_qkvg, w_att_out),
         [SMEM] + [VMEM] * 3,
@@ -359,7 +385,7 @@
 def body(pair, w_proj, w_gate_out, w_out, w_qkvg, w_bias, w_att_out, length):
     rows, count, channels = pair.shape
     share = w_out.shape[0] * rows // count
-    fits = share == rows == 8 and count == channels == w_att_out.shape[0] == 128
+    fits = share == rows == 8 and count // rows == len(ORDERS[0]) and count == channels == w_att_out.shape[0] == 128
     chosen = kernel_body if fits else whole_body
     return chosen(pair, w_proj, w_gate_out, w_out, w_qkvg, w_bias, w_att_out, length)
 

time: 58.6 us -> 52 us (0.89)
  blocking collectives: 51.4 us -> 44.7 us
    all_to_all x3, blocking collectives: 51.4 us -> 44.7 us  [exchange(): lax.all_to_all(x, ('rep', 'dap'), split_axis=0, concat_axis=0, tiled=True...]
where the time goes in v7:
time: 52 us; the launch traced here: 51.8 us
  blocking collectives  44.7 us (86%)
  Pallas kernels  6.29 us (12%)
  between operations  0.71 us (1%)
    all_to_all x3, blocking collectives, exchange(): lax.all_to_all(x, ('rep', 'dap'), split_axis=0, concat_axis=0, tiled=True...  44.7 us
    pallas_call x4, Pallas kernels, call(): pl.pallas_call(kernel, out_shape=[jax.ShapeDtypeStruct(o.shape, o.dtype)...  6.29 us

profile of v7, /device:TPU:0, one launch (start us, length us, event | category | flops | bytes accessed | tf_op | source)
XLA Modules:
  0.0 51.8 jit_solution(4067214333180013433)
XLA Ops:
  0.7 2.1 %shard_map.82 = (bf16[16,128,128]{2,1,0:T(8,128)(2,1)S(1)}, f32[8,128,128]{2,1,0:T(8,128)S(1)}, f32[32,128]{1,0:T(8,128)S(1)}) custom-call(s32[1]{0:T(128)S(6)} %copy.9.length_ref, bf16[8,128,128]{2,1,0:T(8,128)(2,1)} %pair_ref.1, bf16[128,512]{1,0:T(8,128)(2,1)} %w_hbm.1, bf16[128,128]{1,0:T(8,128)(2,1)} %w_gate_hbm.1, bf16[4,128]{1,0:T(4,128)(2,1)} %bitcast.1), custom_call_target="tpu_custom_call" | custom-call | bytes 1491972 | tf_op jit(solution)/shard_map/pallas_call | solution.py:228
  2.8 19.9 %all_to_all.15.came_ref = bf16[16,128,128]{2,1,0:T(8,128)(2,1)S(1)} all-to-all(bf16[16,128,128]{2,1,0:T(8,128)(2,1)S(1)} %get-tuple-element.8), channel_id=1, replica_groups={{8,0,24,16,28,20,12,4,10,2,26,18,30,22,14,6},{13,21,11,5,3,23,31,7,9,17..., dimensions={0} | all-to-all | bytes 1048576 | tf_op jit(solution)/shard_map/all_to_all | solution.py:247
  22.6 0.4 shard_map.83
  23.1 0.0 copy-start
  23.1 0.0 copy-start.2
  23.1 12.9 %all_to_all.16.came_ref = bf16[16,64,128]{2,1,0:T(8,128)(2,1)S(1)} all-to-all(bf16[16,64,128]{2,1,0:T(8,128)(2,1)S(1)} %shard_map.83), channel_id=1, replica_groups={{8,0,24,16,28,20,12,4,10,2,26,18,30,22,14,6},{13,21,11,5,3,23,31,7,9,17..., dimensions={0} | all-to-all | bytes 524288 | tf_op jit(solution)/shard_map/all_to_all | solution.py:247
  36.0 0.0 copy-done
  36.0 0.0 copy-done.2
  36.0 1.1 %shard_map.84 = bf16[16,96,128]{2,1,0:T(8,128)(2,1)S(1)} custom-call(bf16[16,64,128]{2,1,0:T(8,128)(2,1)S(1)} %all_to_all.16.came_ref, f32[8,128,128]{2,1,0:T(8,128)S(1)} %get-tuple-element.9.gate_ref, bf16[8,128,128]{2,1,0:T(8,128)(2,1)S(1)} %copy-done, bf16[128,128]{1,0:T(8,128)(2,1)S(1)} %copy-done.2, f32[32,128]{1,0:T(8,128)S(1)} %get-tuple-element.10.w_rows_ref), custom_call_target="tpu_custom_call" | custom-call | bytes 1490944 | tf_op jit(solution)/shard_map/pallas_call | solution.py:228
  37.1 0.0 copy-start.1
  37.1 0.0 copy-start.3
  37.1 12.0 %all_to_all.17.came_ref = bf16[16,96,128]{2,1,0:T(8,128)(2,1)S(1)} all-to-all(bf16[16,96,128]{2,1,0:T(8,128)(2,1)S(1)} %shard_map.84), channel_id=1, replica_groups={{8,0,24,16,28,20,12,4,10,2,26,18,30,22,14,6},{13,21,11,5,3,23,31,7,9,17..., dimensions={0} | all-to-all | bytes 786432 | tf_op jit(solution)/shard_map/all_to_all | solution.py:247
  49.1 0.0 copy-done.1
  49.1 0.0 copy-done.3
  49.1 2.6 %shard_map.85 = bf16[128,8,128]{2,1,0:T(8,128)(2,1)} custom-call(s32[1]{0:T(128)S(6)} %copy.9.length_ref, bf16[16,96,128]{2,1,0:T(8,128)(2,1)S(1)} %all_to_all.17.came_ref, bf16[128,512]{1,0:T(8,128)(2,1)S(1)} %copy-done.1, bf16[128,128]{1,0:T(8,128)(2,1)S(1)} %copy-done.3), custom_call_target="tpu_custom_call" | custom-call | bytes 819204 | tf_op jit(solution)/shard_map/pallas_call | solution.py:228
Async XLA Ops:
  23.1 12.9 %copy-start = (bf16[8,128,128]{2,1,0:T(8,128)(2,1)S(1)}, bf16[8,128,128]{2,1,0:T(8,128)(2,1)}, u32[]{:S(2)}) copy-start(bf16[8,128,128]{2,1,0:T(8,128)(2,1)} %pair_ref.1) | copy-start | bytes 786436
  23.1 12.9 %copy-start.2 = (bf16[128,128]{1,0:T(8,128)(2,1)S(1)}, bf16[128,128]{1,0:T(8,128)(2,1)}, u32[]{:S(2)}) copy-start(bf16[128,128]{1,0:T(8,128)(2,1)} %w_out_ref.2) | copy-start | bytes 98308
  37.1 12.0 %copy-start.1 = (bf16[128,512]{1,0:T(8,128)(2,1)S(1)}, bf16[128,512]{1,0:T(8,128)(2,1)}, u32[]{:S(2)}) copy-start(bf16[128,512]{1,0:T(8,128)(2,1)} %w_ref.1) | copy-start | bytes 393220
  37.1 12.0 %copy-start.3 = (bf16[128,128]{1,0:T(8,128)(2,1)S(1)}, bf16[128,128]{1,0:T(8,128)(2,1)}, u32[]{:S(2)}) copy-start(bf16[128,128]{1,0:T(8,128)(2,1)} %w_out_ref.3) | copy-start | bytes 98308

commit v8 on v7

--- a/solution.py
+++ b/solution.py
@@ -11,7 +11,6 @@
 SMEM = pl.BlockSpec(memory_space=pltpu.SMEM)
 HBM = pl.BlockSpec(memory_space=pltpu.HBM)
 BF16, F32 = jnp.bfloat16, jnp.float32
-LOG2E = 1.4426950408889634
 ORDERS = [
     [4, 0, 12, 8, 14, 10, 6, 2, 5, 1, 13, 9, 15, 11, 7, 3],
     [6, 10, 5, 2, 1, 11, 15, 3, 4, 8, 12, 0, 14, 7, 13, 9],
@@ -62,21 +61,25 @@
     rows, count, channels = pair_ref.shape
     blocks = out_ref.shape[0]
     hidden = w_ref.shape[1] // 4
+    parts = [pl.ds(start, rows // 2) for start in (0, rows // 2)]
     copies = [
-        pltpu.make_async_copy(pair_hbm, pair_ref, sems.at[0]),
-        pltpu.make_async_copy(w_hbm, w_ref, sems.at[1]),
-        pltpu.make_async_copy(w_gate_hbm, w_gate_ref, sems.at[2]),
-        pltpu.make_async_copy(w_bias_hbm, w_bias_ref, sems.at[3]),
+        pltpu.make_async_copy(pair_hbm.at[parts[0]], pair_ref.at[parts[0]], sems.at[0]),
+        pltpu.make_async_copy(pair_hbm.at[parts[1]], pair_ref.at[parts[1]], sems.at[1]),
+        pltpu.make_async_copy(w_hbm, w_ref, sems.at[2]),
+        pltpu.make_async_copy(w_gate_hbm, w_gate_ref, sems.at[3]),
+        pltpu.make_async_copy(w_bias_hbm, w_bias_ref, sems.at[4]),
     ]
     for copy in copies:
         copy.start()
     first_row = lax.axis_index("dap") * rows
     length = length_ref[0]
     key_valid = jnp.where(lax.broadcasted_iota(jnp.int32, (1, count), 1) < length, 1.0, 0.0)
-    for copy in copies:
+    for r in range(rows):
+        if r % (rows // 2) == 0:
+            copies[r // (rows // 2)].wait()
+        normed_ref[r] = layer_norm(pair_ref[r].astype(F32), 1).astype(BF16)
+    for copy in copies[2:]:
         copy.wait()
-    for r in range(rows):
-        normed_ref[r] = layer_norm(pair_ref[r].astype(F32), 1).astype(BF16)
     w_turned = w_ref[...].T
     for r in range(rows):
         projected = dot(w_turned, normed_ref[r], 1, 1)
@@ -197,17 +200,17 @@
     for h in range(heads):
         own = slice(h * count, (h + 1) * count)
         start = block + h * columns
-        bias = came_ref[:, start : start + columns, :].astype(F32).reshape(count, count) * LOG2E
+        bias = came_ref[:, start : start + columns, :].astype(F32).reshape(count, count)
         own_lanes = jnp.where(lane == h, 1.0, 0.0).astype(BF16)
         for j in range(columns):
-            scaled = dot(k_ref[j] * own_lanes, q_ref[j], 1, 1) * (size ** (-0.5) * LOG2E) + bias
-            score_ref[j, own, :] = jnp.where(valid, scaled, -1000000000.0 * LOG2E)
+            scaled = dot(k_ref[j] * own_lanes, q_ref[j], 1, 1) * size ** (-0.5) + bias
+            score_ref[j, own, :] = jnp.where(valid, scaled, -1000000000.0)
     for h in range(heads):
         own = slice(h * count, (h + 1) * count)
         tops = [jnp.max(score_ref[j, own, :].reshape(-1, 8, count), axis=0) for j in range(columns)]
         tops = [jnp.max(top, axis=0, keepdims=True) for top in tops]
         for j in range(columns):
-            expo_ref[j, own, :] = jnp.exp2(score_ref[j, own, :] - tops[j]).astype(BF16)
+            expo_ref[j, own, :] = jnp.exp(score_ref[j, own, :] - tops[j]).astype(BF16)
     for j in range(columns):
         for h in range(heads):
             own = slice(h * size, (h + 1) * size)
@@ -266,7 +269,7 @@
             pltpu.VMEM(w_gate_out.shape, BF16),
             pltpu.VMEM((heads, channels), BF16),
             pltpu.VMEM(square, BF16),
-            pltpu.SemaphoreType.DMA((4,)),
+            pltpu.SemaphoreType.DMA((5,)),
         ],
     )
     came = exchange(sent, ORDERS)

time: 52 us -> 51.9 us (level)
  no operation moved by 1% of the time
where the time goes in v8:
time: 51.9 us; the launch traced here: 51.7 us
  blocking collectives  44.7 us (86%)
  Pallas kernels  6.21 us (12%)
  between operations  0.71 us (1%)
    all_to_all x3, blocking collectives, exchange(): lax.all_to_all(x, ('rep', 'dap'), split_axis=0, concat_axis=0, tiled=True...  44.7 us
    pallas_call x4, Pallas kernels, call(): pl.pallas_call(kernel, out_shape=[jax.ShapeDtypeStruct(o.shape, o.dtype)...  6.21 us

profile of v8, /device:TPU:0, one launch (start us, length us, event | category | flops | bytes accessed | tf_op | source)
XLA Modules:
  0.0 51.7 jit_solution(16141523634918178785)
XLA Ops:
  0.7 2.0 %shard_map.82 = (bf16[16,128,128]{2,1,0:T(8,128)(2,1)S(1)}, f32[8,128,128]{2,1,0:T(8,128)S(1)}, f32[32,128]{1,0:T(8,128)S(1)}) custom-call(s32[1]{0:T(128)S(6)} %copy.9.length_ref, bf16[8,128,128]{2,1,0:T(8,128)(2,1)} %pair_ref.1, bf16[128,512]{1,0:T(8,128)(2,1)} %w_hbm.1, bf16[128,128]{1,0:T(8,128)(2,1)} %w_gate_hbm.1, bf16[4,128]{1,0:T(4,128)(2,1)} %bitcast.1), custom_call_target="tpu_custom_call" | custom-call | bytes 1491972 | tf_op jit(solution)/shard_map/pallas_call | solution.py:231
  2.6 19.9 %all_to_all.15.came_ref = bf16[16,128,128]{2,1,0:T(8,128)(2,1)S(1)} all-to-all(bf16[16,128,128]{2,1,0:T(8,128)(2,1)S(1)} %get-tuple-element.8), channel_id=1, replica_groups={{8,0,24,16,28,20,12,4,10,2,26,18,30,22,14,6},{13,21,11,5,3,23,31,7,9,17..., dimensions={0} | all-to-all | bytes 1048576 | tf_op jit(solution)/shard_map/all_to_all | solution.py:250
  22.5 0.4 shard_map.83
  22.9 0.0 copy-start
  22.9 0.0 copy-start.2
  23.0 12.9 %all_to_all.16.came_ref = bf16[16,64,128]{2,1,0:T(8,128)(2,1)S(1)} all-to-all(bf16[16,64,128]{2,1,0:T(8,128)(2,1)S(1)} %shard_map.83), channel_id=1, replica_groups={{8,0,24,16,28,20,12,4,10,2,26,18,30,22,14,6},{13,21,11,5,3,23,31,7,9,17..., dimensions={0} | all-to-all | bytes 524288 | tf_op jit(solution)/shard_map/all_to_all | solution.py:250
  35.9 0.0 copy-done
  35.9 0.0 copy-done.2
  35.9 1.1 %shard_map.84 = bf16[16,96,128]{2,1,0:T(8,128)(2,1)S(1)} custom-call(bf16[16,64,128]{2,1,0:T(8,128)(2,1)S(1)} %all_to_all.16.came_ref, f32[8,128,128]{2,1,0:T(8,128)S(1)} %get-tuple-element.9.gate_ref, bf16[8,128,128]{2,1,0:T(8,128)(2,1)S(1)} %copy-done, bf16[128,128]{1,0:T(8,128)(2,1)S(1)} %copy-done.2, f32[32,128]{1,0:T(8,128)S(1)} %get-tuple-element.10.w_rows_ref), custom_call_target="tpu_custom_call" | custom-call | bytes 1490944 | tf_op jit(solution)/shard_map/pallas_call | solution.py:231
  37.0 0.0 copy-start.1
  37.0 0.0 copy-start.3
  37.0 12.0 %all_to_all.17.came_ref = bf16[16,96,128]{2,1,0:T(8,128)(2,1)S(1)} all-to-all(bf16[16,96,128]{2,1,0:T(8,128)(2,1)S(1)} %shard_map.84), channel_id=1, replica_groups={{8,0,24,16,28,20,12,4,10,2,26,18,30,22,14,6},{13,21,11,5,3,23,31,7,9,17..., dimensions={0} | all-to-all | bytes 786432 | tf_op jit(solution)/shard_map/all_to_all | solution.py:250
  49.0 0.0 copy-done.1
  49.0 0.0 copy-done.3
  49.0 2.7 %shard_map.85 = bf16[128,8,128]{2,1,0:T(8,128)(2,1)} custom-call(s32[1]{0:T(128)S(6)} %copy.9.length_ref, bf16[16,96,128]{2,1,0:T(8,128)(2,1)S(1)} %all_to_all.17.came_ref, bf16[128,512]{1,0:T(8,128)(2,1)S(1)} %copy-done.1, bf16[128,128]{1,0:T(8,128)(2,1)S(1)} %copy-done.3), custom_call_target="tpu_custom_call" | custom-call | bytes 819204 | tf_op jit(solution)/shard_map/pallas_call | solution.py:231
Async XLA Ops:
  22.9 12.9 %copy-start = (bf16[8,128,128]{2,1,0:T(8,128)(2,1)S(1)}, bf16[8,128,128]{2,1,0:T(8,128)(2,1)}, u32[]{:S(2)}) copy-start(bf16[8,128,128]{2,1,0:T(8,128)(2,1)} %pair_ref.1) | copy-start | bytes 786436
  22.9 12.9 %copy-start.2 = (bf16[128,128]{1,0:T(8,128)(2,1)S(1)}, bf16[128,128]{1,0:T(8,128)(2,1)}, u32[]{:S(2)}) copy-start(bf16[128,128]{1,0:T(8,128)(2,1)} %w_out_ref.2) | copy-start | bytes 98308
  37.0 12.0 %copy-start.1 = (bf16[128,512]{1,0:T(8,128)(2,1)S(1)}, bf16[128,512]{1,0:T(8,128)(2,1)}, u32[]{:S(2)}) copy-start(bf16[128,512]{1,0:T(8,128)(2,1)} %w_ref.1) | copy-start | bytes 393220
  37.0 12.0 %copy-start.3 = (bf16[128,128]{1,0:T(8,128)(2,1)S(1)}, bf16[128,128]{1,0:T(8,128)(2,1)}, u32[]{:S(2)}) copy-start(bf16[128,128]{1,0:T(8,128)(2,1)} %w_out_ref.3) | copy-start | bytes 98308

commit v9 on v6

--- a/solution.py
+++ b/solution.py
@@ -11,8 +11,7 @@
 SMEM = pl.BlockSpec(memory_space=pltpu.SMEM)
 HBM = pl.BlockSpec(memory_space=pltpu.HBM)
 BF16, F32 = jnp.bfloat16, jnp.float32
-LOG2E = 1.4426950408889634
-ORDER = [4, 0, 12, 8, 14, 10, 6, 2, 5, 1, 13, 9, 15, 11, 7, 3]
+ORDER = [6, 10, 2, 14, 9, 5, 13, 1, 3, 11, 7, 15, 0, 12, 8, 4]
 
 
 def dot(a, b, over_a, over_b):
@@ -59,21 +58,25 @@
     rows, count, channels = pair_ref.shape
     blocks = out_ref.shape[0]
     hidden = w_ref.shape[1] // 4
+    parts = [pl.ds(start, rows // 2) for start in (0, rows // 2)]
     copies = [
-        pltpu.make_async_copy(pair_hbm, pair_ref, sems.at[0]),
-        pltpu.make_async_copy(w_hbm, w_ref, sems.at[1]),
-        pltpu.make_async_copy(w_gate_hbm, w_gate_ref, sems.at[2]),
-        pltpu.make_async_copy(w_bias_hbm, w_bias_ref, sems.at[3]),
+        pltpu.make_async_copy(pair_hbm.at[parts[0]], pair_ref.at[parts[0]], sems.at[0]),
+        pltpu.make_async_copy(pair_hbm.at[parts[1]], pair_ref.at[parts[1]], sems.at[1]),
+        pltpu.make_async_copy(w_hbm, w_ref, sems.at[2]),
+        pltpu.make_async_copy(w_gate_hbm, w_gate_ref, sems.at[3]),
+        pltpu.make_async_copy(w_bias_hbm, w_bias_ref, sems.at[4]),
     ]
     for copy in copies:
         copy.start()
     first_row = lax.axis_index("dap") * rows
     length = length_ref[0]
     key_valid = jnp.where(lax.broadcasted_iota(jnp.int32, (1, count), 1) < length, 1.0, 0.0)
-    for copy in copies:
+    for r in range(rows):
+        if r % (rows // 2) == 0:
+            copies[r // (rows // 2)].wait()
+        normed_ref[r] = layer_norm(pair_ref[r].astype(F32), 1).astype(BF16)
+    for copy in copies[2:]:
         copy.wait()
-    for r in range(rows):
-        normed_ref[r] = layer_norm(pair_ref[r].astype(F32), 1).astype(BF16)
     w_turned = w_ref[...].T
     for r in range(rows):
         projected = dot(w_turned, normed_ref[r], 1, 1)
@@ -186,17 +189,17 @@
     for h in range(heads):
         own = slice(h * count, (h + 1) * count)
         start = block + h * columns
-        bias = came_ref[:, start : start + columns, :].astype(F32).reshape(count, count) * LOG2E
+        bias = came_ref[:, start : start + columns, :].astype(F32).reshape(count, count)
         own_lanes = jnp.where(lane == h, 1.0, 0.0).astype(BF16)
         for j in range(columns):
-            scaled = dot(k_ref[j] * own_lanes, q_ref[j], 1, 1) * (size ** (-0.5) * LOG2E) + bias
-            score_ref[j, own, :] = jnp.where(valid, scaled, -1000000000.0 * LOG2E)
+            scaled = dot(k_ref[j] * own_lanes, q_ref[j], 1, 1) * size ** (-0.5) + bias
+            score_ref[j, own, :] = jnp.where(valid, scaled, -1000000000.0)
     for h in range(heads):
         own = slice(h * count, (h + 1) * count)
         tops = [jnp.max(score_ref[j, own, :].reshape(-1, 8, count), axis=0) for j in range(columns)]
         tops = [jnp.max(top, axis=0, keepdims=True) for top in tops]
         for j in range(columns):
-            expo_ref[j, own, :] = jnp.exp2(score_ref[j, own, :] - tops[j]).astype(BF16)
+            expo_ref[j, own, :] = jnp.exp(score_ref[j, own, :] - tops[j]).astype(BF16)
     for j in range(columns):
         for h in range(heads):
             own = slice(h * size, (h + 1) * size)
@@ -253,7 +256,7 @@
             pltpu.VMEM(w_gate_out.shape, BF16),
             pltpu.VMEM((heads, channels), BF16),
             pltpu.VMEM(square, BF16),
-            pltpu.SemaphoreType.DMA((4,)),
+            pltpu.SemaphoreType.DMA((5,)),
         ],
     )
     came = exchange(sent, ORDER)

time: 53 us -> 51.9 us (0.979)
  blocking collectives: 45.9 us -> 44.9 us
    all_to_all x3, blocking collectives: 45.9 us -> 44.9 us  [exchange(): lax.all_to_all(x, 'dap', split_axis=0, concat_axis=0, tiled=True, axis_in...]
where the time goes in v9:
time: 51.9 us; the launch traced here: 51.7 us
  blocking collectives  44.9 us (87%)
  Pallas kernels  6.08 us (12%)
  between operations  0.71 us (1%)
    all_to_all x3, blocking collectives, exchange(): lax.all_to_all(x, 'dap', split_axis=0, concat_axis=0, tiled=True, axis_in...  44.9 us
    pallas_call x4, Pallas kernels, call(): pl.pallas_call(kernel, out_shape=[jax.ShapeDtypeStruct(o.shape, o.dtype)...  6.08 us

profile of v9, /device:TPU:0, one launch (start us, length us, event | category | flops | bytes accessed | tf_op | source)
XLA Modules:
  0.0 51.7 jit_solution(4314715525385842905)
XLA Ops:
  0.7 2.0 %shard_map.82 = (bf16[16,128,128]{2,1,0:T(8,128)(2,1)S(1)}, f32[8,128,128]{2,1,0:T(8,128)S(1)}, f32[32,128]{1,0:T(8,128)S(1)}) custom-call(s32[1]{0:T(128)S(6)} %copy.9.length_ref, bf16[8,128,128]{2,1,0:T(8,128)(2,1)} %pair_ref.1, bf16[128,512]{1,0:T(8,128)(2,1)} %w_hbm.1, bf16[128,128]{1,0:T(8,128)(2,1)} %w_gate_hbm.1, bf16[4,128]{1,0:T(4,128)(2,1)} %bitcast.1), custom_call_target="tpu_custom_call" | custom-call | bytes 1491972 | tf_op jit(solution)/shard_map/pallas_call | solution.py:220
  2.6 21.6 %all_to_all.15.came_ref = bf16[16,128,128]{2,1,0:T(8,128)(2,1)S(1)} all-to-all(bf16[16,128,128]{2,1,0:T(8,128)(2,1)S(1)} %get-tuple-element.8), channel_id=1, replica_groups={{12,20,4,28,18,10,26,2,6,22,14,30,0,24,16,8},{13,21,5,29,19,11,27,3,7,2..., dimensions={0} | all-to-all | bytes 1048576 | tf_op jit(solution)/shard_map/all_to_all | solution.py:237
  24.2 0.4 shard_map.83
  24.6 0.0 copy-start
  24.7 0.0 copy-start.2
  24.7 10.8 %all_to_all.16.came_ref = bf16[16,64,128]{2,1,0:T(8,128)(2,1)S(1)} all-to-all(bf16[16,64,128]{2,1,0:T(8,128)(2,1)S(1)} %shard_map.83), channel_id=1, replica_groups={{12,20,4,28,18,10,26,2,6,22,14,30,0,24,16,8},{13,21,5,29,19,11,27,3,7,2..., dimensions={0} | all-to-all | bytes 524288 | tf_op jit(solution)/shard_map/all_to_all | solution.py:237
  35.5 0.0 copy-done
  35.5 0.0 copy-done.2
  35.5 1.0 %shard_map.84 = bf16[16,96,128]{2,1,0:T(8,128)(2,1)S(1)} custom-call(bf16[16,64,128]{2,1,0:T(8,128)(2,1)S(1)} %all_to_all.16.came_ref, f32[8,128,128]{2,1,0:T(8,128)S(1)} %get-tuple-element.9.gate_ref, bf16[8,128,128]{2,1,0:T(8,128)(2,1)S(1)} %copy-done, bf16[128,128]{1,0:T(8,128)(2,1)S(1)} %copy-done.2, f32[32,128]{1,0:T(8,128)S(1)} %get-tuple-element.10.w_rows_ref), custom_call_target="tpu_custom_call" | custom-call | bytes 1490944 | tf_op jit(solution)/shard_map/pallas_call | solution.py:220
  36.5 0.0 copy-start.1
  36.5 0.0 copy-start.3
  36.5 12.5 %all_to_all.17.came_ref = bf16[16,96,128]{2,1,0:T(8,128)(2,1)S(1)} all-to-all(bf16[16,96,128]{2,1,0:T(8,128)(2,1)S(1)} %shard_map.84), channel_id=1, replica_groups={{12,20,4,28,18,10,26,2,6,22,14,30,0,24,16,8},{13,21,5,29,19,11,27,3,7,2..., dimensions={0} | all-to-all | bytes 786432 | tf_op jit(solution)/shard_map/all_to_all | solution.py:237
  49.0 0.0 copy-done.1
  49.0 0.0 copy-done.3
  49.0 2.7 %shard_map.85 = bf16[128,8,128]{2,1,0:T(8,128)(2,1)} custom-call(s32[1]{0:T(128)S(6)} %copy.9.length_ref, bf16[16,96,128]{2,1,0:T(8,128)(2,1)S(1)} %all_to_all.17.came_ref, bf16[128,512]{1,0:T(8,128)(2,1)S(1)} %copy-done.1, bf16[128,128]{1,0:T(8,128)(2,1)S(1)} %copy-done.3), custom_call_target="tpu_custom_call" | custom-call | bytes 819204 | tf_op jit(solution)/shard_map/pallas_call | solution.py:220
Async XLA Ops:
  24.6 10.8 %copy-start = (bf16[8,128,128]{2,1,0:T(8,128)(2,1)S(1)}, bf16[8,128,128]{2,1,0:T(8,128)(2,1)}, u32[]{:S(2)}) copy-start(bf16[8,128,128]{2,1,0:T(8,128)(2,1)} %pair_ref.1) | copy-start | bytes 786436
  24.7 10.8 %copy-start.2 = (bf16[128,128]{1,0:T(8,128)(2,1)S(1)}, bf16[128,128]{1,0:T(8,128)(2,1)}, u32[]{:S(2)}) copy-start(bf16[128,128]{1,0:T(8,128)(2,1)} %w_out_ref.2) | copy-start | bytes 98308
  36.5 12.5 %copy-start.1 = (bf16[128,512]{1,0:T(8,128)(2,1)S(1)}, bf16[128,512]{1,0:T(8,128)(2,1)}, u32[]{:S(2)}) copy-start(bf16[128,512]{1,0:T(8,128)(2,1)} %w_ref.1) | copy-start | bytes 393220
  36.5 12.5 %copy-start.3 = (bf16[128,128]{1,0:T(8,128)(2,1)S(1)}, bf16[128,128]{1,0:T(8,128)(2,1)}, u32[]{:S(2)}) copy-start(bf16[128,128]{1,0:T(8,128)(2,1)} %w_out_ref.3) | copy-start | bytes 98308

commit v10 on v9

--- a/solution.py
+++ b/solution.py
@@ -11,7 +11,7 @@
 SMEM = pl.BlockSpec(memory_space=pltpu.SMEM)
 HBM = pl.BlockSpec(memory_space=pltpu.HBM)
 BF16, F32 = jnp.bfloat16, jnp.float32
-ORDER = [6, 10, 2, 14, 9, 5, 13, 1, 3, 11, 7, 15, 0, 12, 8, 4]
+ORDER = [11, 10, 3, 14, 0, 2, 13, 1, 9, 12, 8, 4, 5, 6, 7, 15]
 
 
 def dot(a, b, over_a, over_b):

time: 51.9 us -> 51 us (0.983)
  blocking collectives: 44.9 us -> 43.9 us
    all_to_all x3, blocking collectives: 44.9 us -> 43.9 us  [exchange(): lax.all_to_all(x, 'dap', split_axis=0, concat_axis=0, tiled=True, axis_in...]
where the time goes in v10:
time: 51 us; the launch traced here: 50.7 us
  blocking collectives  43.9 us (86%)
  Pallas kernels  6.07 us (12%)
  between operations  0.71 us (1%)
    all_to_all x3, blocking collectives, exchange(): lax.all_to_all(x, 'dap', split_axis=0, concat_axis=0, tiled=True, axis_in...  43.9 us
    pallas_call x4, Pallas kernels, call(): pl.pallas_call(kernel, out_shape=[jax.ShapeDtypeStruct(o.shape, o.dtype)...  6.07 us

profile of v10, /device:TPU:0, one launch (start us, length us, event | category | flops | bytes accessed | tf_op | source)
XLA Modules:
  0.0 50.7 jit_solution(1149704486913801673)
XLA Ops:
  0.7 2.0 %shard_map.82 = (bf16[16,128,128]{2,1,0:T(8,128)(2,1)S(1)}, f32[8,128,128]{2,1,0:T(8,128)S(1)}, f32[32,128]{1,0:T(8,128)S(1)}) custom-call(s32[1]{0:T(128)S(6)} %copy.9.length_ref, bf16[8,128,128]{2,1,0:T(8,128)(2,1)} %pair_ref.1, bf16[128,512]{1,0:T(8,128)(2,1)} %w_hbm.1, bf16[128,128]{1,0:T(8,128)(2,1)} %w_gate_hbm.1, bf16[4,128]{1,0:T(4,128)(2,1)} %bitcast.1), custom_call_target="tpu_custom_call" | custom-call | bytes 1491972 | tf_op jit(solution)/shard_map/pallas_call | solution.py:220
  2.6 20.1 %all_to_all.15.came_ref = bf16[16,128,128]{2,1,0:T(8,128)(2,1)S(1)} all-to-all(bf16[16,128,128]{2,1,0:T(8,128)(2,1)S(1)} %get-tuple-element.8), channel_id=1, replica_groups={{22,20,6,28,0,4,26,2,18,24,16,8,10,12,14,30},{23,21,7,29,1,5,27,3,19,25..., dimensions={0} | all-to-all | bytes 1048576 | tf_op jit(solution)/shard_map/all_to_all | solution.py:237
  22.7 0.4 shard_map.83
  23.1 0.0 copy-start
  23.2 0.0 copy-start.2
  23.2 11.7 %all_to_all.16.came_ref = bf16[16,64,128]{2,1,0:T(8,128)(2,1)S(1)} all-to-all(bf16[16,64,128]{2,1,0:T(8,128)(2,1)S(1)} %shard_map.83), channel_id=1, replica_groups={{22,20,6,28,0,4,26,2,18,24,16,8,10,12,14,30},{23,21,7,29,1,5,27,3,19,25..., dimensions={0} | all-to-all | bytes 524288 | tf_op jit(solution)/shard_map/all_to_all | solution.py:237
  34.8 0.0 copy-done
  34.8 0.0 copy-done.2
  34.9 1.0 %shard_map.84 = bf16[16,96,128]{2,1,0:T(8,128)(2,1)S(1)} custom-call(bf16[16,64,128]{2,1,0:T(8,128)(2,1)S(1)} %all_to_all.16.came_ref, f32[8,128,128]{2,1,0:T(8,128)S(1)} %get-tuple-element.9.gate_ref, bf16[8,128,128]{2,1,0:T(8,128)(2,1)S(1)} %copy-done, bf16[128,128]{1,0:T(8,128)(2,1)S(1)} %copy-done.2, f32[32,128]{1,0:T(8,128)S(1)} %get-tuple-element.10.w_rows_ref), custom_call_target="tpu_custom_call" | custom-call | bytes 1490944 | tf_op jit(solution)/shard_map/pallas_call | solution.py:220
  35.8 0.0 copy-start.1
  35.9 0.0 copy-start.3
  35.9 12.2 %all_to_all.17.came_ref = bf16[16,96,128]{2,1,0:T(8,128)(2,1)S(1)} all-to-all(bf16[16,96,128]{2,1,0:T(8,128)(2,1)S(1)} %shard_map.84), channel_id=1, replica_groups={{22,20,6,28,0,4,26,2,18,24,16,8,10,12,14,30},{23,21,7,29,1,5,27,3,19,25..., dimensions={0} | all-to-all | bytes 786432 | tf_op jit(solution)/shard_map/all_to_all | solution.py:237
  48.1 0.0 copy-done.1
  48.1 0.0 copy-done.3
  48.1 2.7 %shard_map.85 = bf16[128,8,128]{2,1,0:T(8,128)(2,1)} custom-call(s32[1]{0:T(128)S(6)} %copy.9.length_ref, bf16[16,96,128]{2,1,0:T(8,128)(2,1)S(1)} %all_to_all.17.came_ref, bf16[128,512]{1,0:T(8,128)(2,1)S(1)} %copy-done.1, bf16[128,128]{1,0:T(8,128)(2,1)S(1)} %copy-done.3), custom_call_target="tpu_custom_call" | custom-call | bytes 819204 | tf_op jit(solution)/shard_map/pallas_call | solution.py:220
Async XLA Ops:
  23.1 11.7 %copy-start = (bf16[8,128,128]{2,1,0:T(8,128)(2,1)S(1)}, bf16[8,128,128]{2,1,0:T(8,128)(2,1)}, u32[]{:S(2)}) copy-start(bf16[8,128,128]{2,1,0:T(8,128)(2,1)} %pair_ref.1) | copy-start | bytes 786436
  23.2 11.7 %copy-start.2 = (bf16[128,128]{1,0:T(8,128)(2,1)S(1)}, bf16[128,128]{1,0:T(8,128)(2,1)}, u32[]{:S(2)}) copy-start(bf16[128,128]{1,0:T(8,128)(2,1)} %w_out_ref.2) | copy-start | bytes 98308
  35.8 12.2 %copy-start.1 = (bf16[128,512]{1,0:T(8,128)(2,1)S(1)}, bf16[128,512]{1,0:T(8,128)(2,1)}, u32[]{:S(2)}) copy-start(bf16[128,512]{1,0:T(8,128)(2,1)} %w_ref.1) | copy-start | bytes 393220
  35.9 12.2 %copy-start.3 = (bf16[128,128]{1,0:T(8,128)(2,1)S(1)}, bf16[128,128]{1,0:T(8,128)(2,1)}, u32[]{:S(2)}) copy-start(bf16[128,128]{1,0:T(8,128)(2,1)} %w_out_ref.3) | copy-start | bytes 98308
